TPU v7x, 256 devices: a whole 4x4x8 slice. The times are simulated.
256 devices in a mesh: ctx: 16 (over y, x_hi, core), tp: 16 (over x_lo, z).
Axes of the slice: x: 4 (x_hi: 2, x_lo: 2; x = x_hi * 2 + x_lo), y: 4, z: 8, core: 2. Of those that a mesh axis runs over, the one named last changes fastest.
Arguments:
- prompt_hidden: bfloat16 [1024, 16384], P('ctx', 'tp'), may hold values from -6 to 6
- kv_weight: bfloat16 [16384, 2048], P('tp'), may hold values from -0.046875 to 0.046875
- cache_k: bfloat16 [16384, 1024], P('ctx'), may hold values from -24 to 24
- cache_v: bfloat16 [16384, 1024], P('ctx'), may hold values from -6 to 6
- prompt_q: bfloat16 [1024, 16384], P('ctx', 'tp'), may hold values from -24 to 24
- dec_q: bfloat16 [128, 16384], P('ctx', 'tp'), may hold values from -24 to 24
- dec_k: bfloat16 [128, 1024], P('ctx'), may hold values from -6 to 6
- dec_v: bfloat16 [128, 1024], P('ctx'), may hold values from -6 to 6
- cache_lengths: int32 [16], P('ctx'), may hold values from 1 to 1024, 8192 in all
- prompt_pos: int32 [1024], P('ctx'), may hold values from 0 to 1023, each once
- dec_owner: int32 [128], P('ctx'), may hold values from 0 to 15
Outputs:
- prompt_out: bfloat16 [1024, 16384], P('ctx', 'tp')
- dec_out: bfloat16 [128, 16384], P('ctx', 'tp')
Inputs may be any that keep to these rules, and one draw needn't show every extreme that they name: `prompt_pos`: a permutation of the prompt positions.
All inputs are finite; a program needn't handle non-finite values. No bound on the sum of `cache_lengths` on one device may be relied on, other than what follows from the above.
Results may differ from a plain program's by a relative error of at most 0.022.
Values may be sent and summed in bfloat16 or wider, within the bound.
No kernel may reach another device: no remote copies, remote signals or barrier semaphores. Data moves between devices by JAX's collectives and lax.ppermute only.
A program may use at most 128 MiB of HBM per device.

v0:
```python
import functools
import math

import jax
import jax.numpy as jnp
from jax import lax
from jax.experimental import pallas as pl
from jax.experimental.pallas import tpu as pltpu
from jax.sharding import PartitionSpec as P

HD = 128
HEADS = 8
KVH = 8
ROWS = 64
DROWS = 8
PR = HEADS * ROWS
QR = PR + HEADS * DROWS
MSG = QR + 16
SLOTS = 1024
CHUNK = 256
EXP = HD ** -0.5 * math.log2(math.e)
MASKED = -1e30
FLOOR = -1e20
BASE = 32
F32 = jnp.float32
BF16 = jnp.bfloat16


def swap(f):
    out = []
    for i in range(256):
        y, xh, core, xl, z = i // 64, i // 32 % 2, i // 16 % 2, i // 8 % 2, i % 8
        y, xh, core, xl, z = f(y, xh, core, xl, z)
        out.append((i, (((y * 2 + xh) * 2 + core) * 2 + xl) * 8 + z))
    return out


CORE = swap(lambda y, xh, c, xl, z: (y, xh, 1 - c, xl, z))
XADJ = swap(lambda y, xh, c, xl, z: (y, 1 - xh, c, 1 - xl, z))
XFAR = swap(lambda y, xh, c, xl, z: (y, 1 - xh, c, xl, z))
XLOW = swap(lambda y, xh, c, xl, z: (y, xh, c, 1 - xl, z))
Y1, Y2, Y3 = (swap(lambda y, xh, c, xl, z, k=k: (y ^ k, xh, c, xl, z)) for k in (1, 2, 3))
Z1, Z2, Z6 = (swap(lambda y, xh, c, xl, z, k=k: (y, xh, c, xl, z ^ k)) for k in (1, 2, 6))


def tie(x, *others):
    return lax.optimization_barrier((x, *others))[0]


def move(x, pairs):
    return lax.ppermute(x, ("ctx", "tp"), pairs)


def vmem(mib):
    return pltpu.CompilerParams(vmem_limit_bytes=mib * 1024 * 1024)


PARTS = 4
KV = 2 * SLOTS + 16
PIECE = 2 * ROWS + 16
PAIR = 2 * PIECE


def project_kernel(tp, hidden, weight, send, keep, h, w, acc, sem_w, sem_h):
    side = tp[0] // 8
    deep = hidden.shape[1] // PARTS
    copy = pltpu.make_async_copy
    copy_h = copy(hidden, h, sem_h)
    copies = [
        copy(weight.at[pl.ds(i * deep, deep)], w.at[pl.ds(i * deep, deep)], sem_w.at[i]) for i in range(PARTS)
    ]
    copy_h.start()
    for x in copies:
        x.start()
    copy_h.wait()
    for i in range(PARTS):
        copies[i].wait()
        part = slice(i * deep, (i + 1) * deep)
        product = jnp.dot(h[:, part], w[part, :], preferred_element_type=F32)
        acc[...] = product if i == 0 else acc[...] + product
    for i in range(4):
        for out, where in ((send, 1 - side), (keep, side)):
            at = (where * 4 + i) * HD
            for v in range(2):
                block = acc[:, pl.ds(pl.multiple_of(at + v * KVH * HD, HD), HD)]
                out[i, v * ROWS:(v + 1) * ROWS, :] = block.astype(out.dtype)


def far_call(kernel, scalars, arrays, outs, scratch, name):
    whole = pl.BlockSpec(memory_space=pltpu.VMEM)
    return pl.pallas_call(
        kernel,
        in_specs=[pl.BlockSpec(memory_space=pltpu.SMEM)] * len(scalars)
        + [pl.BlockSpec(memory_space=pl.ANY)] * len(arrays),
        out_specs=[whole] * len(outs),
        out_shape=[jax.ShapeDtypeStruct(shape, dtype) for shape, dtype in outs],
        scratch_shapes=scratch,
        compiler_params=vmem(12),
        name=name,
    )(*scalars, *[pltpu.with_memory_space_constraint(x, pltpu.HBM) for x in arrays])


def project(tp, hidden, weight):
    feats, width = weight.shape
    half = (4, 2 * ROWS, HD)
    scratch = [
        pltpu.VMEM((ROWS, feats), BF16),
        pltpu.VMEM((feats, width), BF16),
        pltpu.VMEM((ROWS, width), F32),
        pltpu.SemaphoreType.DMA((PARTS,)),
        pltpu.SemaphoreType.DMA,
    ]
    return far_call(project_kernel, (tp,), (hidden, weight), [(half, BF16), (half, F32)], scratch, "project")


def pack_kernel(
    tp, lengths, owner, pos, cache_k, cache_v, prompt_q, dec_q, dec_k, dec_v,
    kv_own, kv_give, q_own, own_kv, pos_line, pos_column,
    c, pq, dq, dkv, owner_s, pos_s, sem_c, sem_s,
):
    head = tp[0] // 2
    own = pl.ds(pl.multiple_of(head * HD, HD), HD)
    other = pl.ds(pl.multiple_of((head ^ 4) * HD, HD), HD)
    copy = pltpu.make_async_copy
    copies = [
        copy(source, target, sem_s.at[i])
        for i, (source, target) in enumerate((
            (owner, owner_s), (pos, pos_s), (prompt_q, pq), (dec_q, dq),
            (dec_k.at[:, own], dkv.at[0]), (dec_v.at[:, own], dkv.at[1]),
        ))
    ]
    copies_c = [
        copy(source.at[:, part], c.at[i], sem_c.at[i])
        for i, (source, part) in enumerate(
            ((cache_k, other), (cache_v, other), (cache_k, own), (cache_v, own))
        )
    ]
    for x in copies + copies_c:
        x.start()
    for x in copies:
        x.wait()
    for j in range(HEADS):
        q_own[j * ROWS:(j + 1) * ROWS, :] = pq[:, j * HD:(j + 1) * HD]
    d = dq[...].astype(F32)
    rows = jnp.concatenate([d[:, j * HD:(j + 1) * HD] for j in range(HEADS)], 0)
    q_own[PR:QR, :] = rows.astype(BF16)
    row = lax.broadcasted_iota(jnp.int32, (16, HD), 0)
    who = jnp.zeros((16, HD), jnp.int32)
    for r in range(DROWS):
        who = jnp.where(row == r, owner_s[r], who)
    q_own[QR:MSG, :] = who.astype(F32).astype(BF16)
    lane = lax.broadcasted_iota(jnp.int32, (16, HD), 1) % ROWS
    eight = lax.broadcasted_iota(jnp.int32, (DROWS, HD), 0)
    line = jnp.zeros((16, HD), jnp.int32)
    for b in range(ROWS // DROWS):
        column = jnp.zeros((DROWS, HD), jnp.int32)
        for r in range(DROWS):
            column = jnp.where(eight == r, pos_s[b * DROWS + r], column)
            line = jnp.where(lane == b * DROWS + r, pos_s[b * DROWS + r], line)
        pos_column[b * DROWS:(b + 1) * DROWS, :] = column.astype(F32)
    line = jnp.where(row == 0, line // BASE, jnp.where(row == 1, line % BASE, 0))
    pos_line[...] = line.astype(F32).astype(BF16)
    own_kv[0:DROWS, :] = dkv[0].astype(F32)
    own_kv[DROWS:2 * DROWS, :] = dkv[1].astype(F32)

    n = lengths[0]
    value = jnp.where(row < 8, n // BASE, n % BASE).astype(F32).astype(BF16)
    filled = lax.broadcasted_iota(jnp.int32, (SLOTS, HD), 0) < n
    for i, out in enumerate((kv_give, kv_own)):
        copies_c[2 * i].wait()
        copies_c[2 * i + 1].wait()
        keys = c[2 * i].astype(F32)
        out[0:SLOTS, :] = jnp.where(filled, keys, keys[0:1]).astype(BF16)
        out[SLOTS:2 * SLOTS, :] = jnp.where(filled, c[2 * i + 1].astype(F32), 0.0).astype(BF16)
        out[2 * SLOTS:KV, :] = value


def pack(tp, lengths, *arrays):
    outs = [((KV, HD), BF16), ((KV, HD), BF16), ((MSG, HD), BF16), ((2 * DROWS, HD), F32), ((16, HD), BF16), ((ROWS, HD), F32)]
    scratch = [
        pltpu.VMEM((4, SLOTS, HD), BF16),
        pltpu.VMEM((ROWS, HEADS * HD), BF16),
        pltpu.VMEM((DROWS, HEADS * HD), BF16),
        pltpu.VMEM((2, DROWS, HD), BF16),
        pltpu.SMEM((DROWS,), jnp.int32),
        pltpu.SMEM((ROWS,), jnp.int32),
        pltpu.SemaphoreType.DMA((4,)),
        pltpu.SemaphoreType.DMA((6,)),
    ]
    return far_call(pack_kernel, (tp, lengths), arrays, outs, scratch, "pack")


def glue(kernel, scalars, arrays, outs, name):
    whole = pl.BlockSpec(memory_space=pltpu.VMEM)
    return pl.pallas_call(
        kernel,
        in_specs=[pl.BlockSpec(memory_space=pltpu.SMEM)] * len(scalars) + [whole] * len(arrays),
        out_specs=[whole] * len(outs),
        out_shape=[jax.ShapeDtypeStruct(shape, dtype) for shape, dtype in outs],
        compiler_params=vmem(4),
        name=name,
    )(*scalars, *arrays)


def halve_kernel(bit, tp, keep, got, send, left):
    half = send.shape[0]
    mine = tp[0] // bit % 2
    for i in range(half):
        j = (1 - mine) * half + i
        send[i] = (keep[j] + got[j].astype(F32)).astype(BF16)
        j = mine * half + i
        left[i] = keep[j] + got[j].astype(F32)


def halve(bit, tp, keep, got):
    shape = (keep.shape[0] // 2,) + keep.shape[1:]
    return glue(functools.partial(halve_kernel, bit), (tp,), (keep, got), ((shape, BF16), (shape, F32)), "halve")


def add_kernel(keep, got, send, total):
    x = keep[0] + got[0].astype(F32)
    send[...] = x.astype(BF16)
    total[...] = x


def join_kernel(total, got, line, piece):
    piece[0:2 * ROWS, :] = (total[...] + got[...].astype(F32)).astype(BF16)
    piece[2 * ROWS:PIECE, :] = line[...]


def letters_kernel(piece, got, back1, back2, back3, out1, out2, out3):
    for back, out in ((back1, out1), (back2, out2), (back3, out3)):
        out[0:PIECE, :] = piece[...]
        out[PIECE:PAIR, :] = got[...]
        out[PAIR:PAIR + MSG, :] = back[...]


def near_kernel(piece, got, m1, m2, m3, out):
    out[0:PIECE, :] = piece[...]
    out[PIECE:PAIR, :] = got[...]
    for i, m in enumerate((m1, m2, m3)):
        out[(i + 1) * PAIR:(i + 2) * PAIR, :] = m[0:PAIR, :]


BLOCK = 192


def absorb(ctx, n, kv, qs, acc, top):
    tail = kv[2 * SLOTS:2 * SLOTS + 16, :].astype(F32)
    length = jnp.max(tail[:8] * BASE + tail[8:]).astype(jnp.int32)
    host = (ctx[0] ^ n).astype(F32)

    def chunk(base, size):
        k = kv[pl.ds(pl.multiple_of(base, 256), size), :]
        v = kv[pl.ds(pl.multiple_of(SLOTS + base, 256), size), :]
        one = lax.broadcasted_iota(jnp.int32, (size, HD), 0) < length - base
        v = jnp.concatenate([v, jnp.where(one, 1.0, 0.0).astype(BF16)], 1)
        for g, q in enumerate(qs):
            for start in range(0, QR, BLOCK):
                rows = slice(g * QR + start, g * QR + start + BLOCK)
                s = lax.dot_general(
                    q[start:start + BLOCK, :], k, (((1,), (1,)), ((), ())), preferred_element_type=F32
                )
                old = top[rows, :]
                new = jnp.maximum(old, jnp.max(s, axis=1, keepdims=True))
                less = new
                if start + BLOCK > PR:
                    owner = q[QR:MSG, :].astype(F32)[:DROWS]
                    owner = jnp.concatenate([jnp.full((BLOCK - QR + PR, HD), 99.0)] + [owner] * HEADS, 0)
                    seen = owner >= host
                    new = jnp.where(seen, new, old)
                    less = jnp.where(seen, new, -MASKED)
                p = jnp.exp2((s - jnp.concatenate([less] * (size // HD), 1)) * EXP)
                shrink = jnp.exp2((old - new) * EXP)
                acc[rows, :] = acc[rows, :] * jnp.concatenate([shrink, shrink], 1) + jnp.dot(
                    p.astype(BF16), v, preferred_element_type=F32
                )
                top[rows, :] = new

    rest = length % 512
    full = length // 512 + (rest > 256).astype(jnp.int32)

    def step(c, carry):
        chunk(c * 512, 512)
        return carry

    lax.fori_loop(0, full, step, 0)

    @pl.when((rest > 0) & (rest <= 256))
    def _():
        chunk(full * 512, 256)


def first_kernel(ctx, q0, q1, kv0, kv1, acc, top):
    acc[...] = jnp.zeros_like(acc)
    top[...] = jnp.full_like(top, FLOOR)
    for n, kv in enumerate((kv0, kv1)):
        absorb(ctx, n, kv, (q0, q1), acc, top)


def second_kernel(ctx, q0, q1, kv2, kv3, acc0, top0, out0, out1, acc, top):
    acc[...] = acc0[...]
    top[...] = top0[...]
    for n, kv in enumerate((kv2, kv3)):
        absorb(ctx, n + 2, kv, (q0, q1), acc, top)
    diagonal = lax.broadcasted_iota(jnp.int32, (HD, HD), 0) == lax.broadcasted_iota(jnp.int32, (HD, HD), 1)
    index = lax.broadcasted_iota(jnp.int32, (16, HD), 0)
    for g, out in enumerate((out0, out1)):
        rows = slice(g * QR, (g + 1) * QR)
        total = acc[rows, HD:]
        some = total > 0.0
        total = jnp.where(some, total, 1.0)
        out[0:QR, :] = jnp.where(some, acc[rows, :HD] / total, 0.0).astype(BF16)
        level = jnp.where(some, top[rows, :] * EXP + jnp.log2(total), FLOOR)
        packed = jnp.zeros((16, HD), F32)
        for b in range(5):
            block = level[b * HD:(b + 1) * HD, :]
            if b == 4:
                block = jnp.concatenate([block, jnp.zeros((HD - QR + PR, HD), F32)], 0)
            line = jnp.sum(jnp.where(diagonal, block, 0.0), axis=0, keepdims=True)
            for i in range(3):
                piece = line.astype(BF16).astype(F32)
                packed = jnp.where(index == 3 * b + i, piece, packed)
                line = line - piece
        out[QR:MSG, :] = packed.astype(BF16)


STATE = ((2 * QR, 2 * HD), (2 * QR, HD))


def cache_call(kernel, host, arrays, outs, scratch, name):
    whole = pl.BlockSpec(memory_space=pltpu.VMEM)
    return pl.pallas_call(
        kernel,
        in_specs=[pl.BlockSpec(memory_space=pltpu.SMEM)] + [whole] * len(arrays),
        out_specs=[whole] * len(outs),
        out_shape=[jax.ShapeDtypeStruct(shape, dtype) for shape, dtype in outs],
        scratch_shapes=[pltpu.VMEM(shape, F32) for shape in scratch],
        compiler_params=vmem(8),
        name=name,
    )(host, *arrays)


def cache_first(host, qs, kvs):
    return cache_call(first_kernel, host, (*qs, *kvs), [(x, F32) for x in STATE], (), "cache_first")


def cache_second(host, qs, kvs, state):
    return cache_call(
        second_kernel, host, (*qs, *kvs, *state), [((MSG, HD), BF16)] * 2, STATE, "cache_second"
    )


NEAR = 8


def lay_out(ref, keys, vals):
    vals[:, HD:] = jnp.ones((NEAR * ROWS, HD), BF16)
    lane = lax.broadcasted_iota(jnp.int32, (1, HD), 1)
    lines = []
    for i in range(NEAR):
        at = i * ROWS
        base = i * PIECE
        keys[at:at + ROWS, :] = ref[base:base + ROWS, :]
        vals[at:at + ROWS, 0:HD] = ref[base + ROWS:base + 2 * ROWS, :]
        tail = ref[base + 2 * ROWS:base + PIECE, :].astype(F32)
        lines.append(tail[0:1] * BASE + tail[1:2])
    return jnp.concatenate(
        [jnp.where(lane < ROWS, lines[2 * i], lines[2 * i + 1]) for i in range(NEAR // 2)], 1
    )


def prompt_part(q, mask, keys, vals):
    s = lax.dot_general(q, keys[...], (((1,), (1,)), ((), ())), preferred_element_type=F32)
    s = jnp.where(mask, s, MASKED)
    high = jnp.maximum(jnp.max(s, axis=1, keepdims=True), FLOOR)
    p = jnp.exp2((s - high) * EXP)
    o = jnp.dot(p.astype(BF16), vals[...], preferred_element_type=F32)
    return high * EXP, o[:, HD:], o[:, :HD]


def middle_kernel(q, m0, m1, m2, m3, near, own_kv, pos, out_d, value, level, keys, vals):
    parts = ((m0, 0), (m1, PAIR), (m2, PAIR), (m3, PAIR))
    where = lay_out(near, keys, vals)
    diagonal = lax.broadcasted_iota(jnp.int32, (HD, HD), 0) == lax.broadcasted_iota(jnp.int32, (HD, HD), 1)

    def column(ref, base, b):
        tail = ref[base + QR:base + MSG, :].astype(F32)
        line = tail[3 * b:3 * b + 1] + tail[3 * b + 1:3 * b + 2] + tail[3 * b + 2:3 * b + 3]
        return jnp.sum(jnp.where(diagonal, line, 0.0), axis=1, keepdims=True)

    def merge(b, size, top, total, summed):
        tops = [column(ref, base, b)[:size] for ref, base in parts]
        high = functools.reduce(jnp.maximum, tops, top)
        weight = jnp.exp2(top - high)
        summed, total = weight * summed, weight * total
        for x, (ref, base) in zip(tops, parts):
            weight = jnp.exp2(x - high)
            summed = summed + weight * ref[base + b * HD:base + b * HD + size, :].astype(F32)
            total = total + weight
        return summed / total, high + jnp.log2(total)

    mine = jnp.concatenate([pos[...], pos[...]], 0)[:, 0:1]
    mask = where <= mine
    for b in range(4):
        rows = slice(b * HD, (b + 1) * HD)
        got, high = merge(b, HD, *prompt_part(q[rows, :], mask, keys, vals))
        value[rows, :] = got
        level[rows, :] = high
    key = jnp.concatenate([own_kv[0:DROWS, :]] * HEADS, 0)
    own = jnp.concatenate([own_kv[DROWS:2 * DROWS, :]] * HEADS, 0)
    top = jnp.sum(q[PR:QR, :].astype(F32) * key, axis=1, keepdims=True) * EXP
    got, high = merge(4, QR - PR, top, jnp.ones((QR - PR, HD), F32), own)
    for j in range(HEADS):
        out_d[:, j * HD:(j + 1) * HD] = got[j * DROWS:(j + 1) * DROWS].astype(BF16)


def final_kernel(q, far, value, level, pos, out_p, keys, vals):
    where = lay_out(far, keys, vals)
    mine = jnp.concatenate([pos[...], pos[...]], 0)[:, 0:1]
    mask = where <= mine
    for b in range(4):
        rows = slice(b * HD, (b + 1) * HD)
        top, total, summed = prompt_part(q[rows, :], mask, keys, vals)
        before = level[rows, :]
        high = jnp.maximum(top, before)
        left, right = jnp.exp2(before - high), jnp.exp2(top - high)
        merged = ((left * value[rows, :] + right * summed) / (left + right * total)).astype(BF16)
        out_p[:, 2 * b * HD:(2 * b + 1) * HD] = merged[:ROWS]
        out_p[:, (2 * b + 1) * HD:(2 * b + 2) * HD] = merged[ROWS:]


def last_call(kernel, arrays, outs, name):
    whole = pl.BlockSpec(memory_space=pltpu.VMEM)
    return pl.pallas_call(
        kernel,
        in_specs=[whole] * len(arrays),
        out_specs=[whole] * len(outs),
        out_shape=[jax.ShapeDtypeStruct(shape, dtype) for shape, dtype in outs],
        scratch_shapes=[pltpu.VMEM((NEAR * ROWS, HD), BF16), pltpu.VMEM((NEAR * ROWS, 2 * HD), BF16)],
        compiler_params=vmem(8),
        name=name,
    )(*arrays)


def body(
    prompt_hidden, kv_weight, cache_k, cache_v, prompt_q, dec_q, dec_k, dec_v,
    cache_lengths, prompt_pos, dec_owner,
):
    host = lax.axis_index("ctx").reshape(1)
    tp = lax.axis_index("tp").reshape(1)
    send, keep = project(tp, prompt_hidden, kv_weight)
    got = move(send, XLOW)
    kv_own, kv_give, q_own, own_kv, line, pos = pack(
        tie(tp, send), cache_lengths, dec_owner, prompt_pos, cache_k, cache_v, prompt_q, dec_q, dec_k, dec_v
    )
    kv_adj = move(kv_give, XADJ)
    kv_core = move(kv_own, CORE)
    q1 = move(q_own, Y1)
    q3 = move(q_own, Y3)

    send, keep = halve(4, tp, keep, got)
    got = move(send, Z6)
    q2 = move(tie(q_own, send), Y2)
    groups = ((q_own, q1), (q2, q3))
    state0 = cache_first(tie(host, send), groups[0], [kv_own, kv_core])
    got = tie(got, *state0)
    send, keep = halve(2, tp, keep, got)
    got = move(send, Z2)
    state1 = cache_first(tie(host, send), groups[1], [kv_own, kv_core])
    got = tie(got, kv_adj, *state1)
    half = (2 * ROWS, HD)
    send, total = glue(add_kernel, (), (keep, got), ((half, BF16), (half, F32)), "add")
    got = move(send, Z1)
    kv_diag = move(tie(kv_adj, send), CORE)
    back0 = cache_second(tie(host, send), groups[0], [kv_adj, kv_diag], state0)
    got = tie(got, *back0)
    piece, = glue(join_kernel, (), (total, got, line), (((PIECE, HD), BF16),), "join")
    got = move(piece, XFAR)
    back1 = cache_second(tie(host, piece), groups[1], [kv_adj, kv_diag], state1)
    got = tie(got, *back1)
    letter = ((PAIR + MSG, HD), BF16)
    letters = glue(letters_kernel, (), (piece, got, back0[1], *back1), (letter,) * 3, "letters")
    parts = [move(x, pairs) for x, pairs in zip(letters, (Y1, Y2, Y3))]
    near, = glue(near_kernel, (), (piece, got, *parts), (((4 * PAIR, HD), BF16),), "near")
    far = move(near, CORE)
    out_d, value, level = last_call(
        middle_kernel, (q_own, back0[0], *parts, near, own_kv, pos),
        [((DROWS, HEADS * HD), BF16), ((PR, HD), F32), ((PR, HD), F32)], "middle",
    )
    far = tie(far, level)
    out_p, = last_call(
        final_kernel, (q_own, far, value, level, pos), [((ROWS, HEADS * HD), BF16)], "final"
    )
    return out_p, out_d


def solution(mesh):
    in_specs = (
        P("ctx", "tp"), P("tp", None), P("ctx", None), P("ctx", None), P("ctx", "tp"),
        P("ctx", "tp"), P("ctx", None), P("ctx", None), P("ctx"), P("ctx"), P("ctx"),
    )
    out_specs = (P("ctx", "tp"), P("ctx", "tp"))
    return jax.shard_map(body, mesh=mesh, in_specs=in_specs, out_specs=out_specs, check_vma=False)
```

profile of v0, /device:TPU:1, one launch (start us, length us, event | category | flops | bytes accessed | tf_op | source)
XLA Modules:
  0.0 65.7 jit_solution(5835772011453021038)
XLA Ops:
  1.3 2.9 %project.1 = (bf16[4,128,128]{2,1,0:T(8,128)(2,1)S(1)}, f32[4,128,128]{2,1,0:T(8,128)S(1)}) custom-call(s32[1]{0:T(128)} %bitcast.tp, bf16[64,1024]{1,0:T(8,128)(2,1)} %hidden.1, bf16[1024,2048]{1,0:T(8,128)(2,1)} %weight.1), custom_call_target="tpu_custom_call" | custom-call | tf_op jit(solution)/shard_map/project/pallas_call | solution.py:91
  4.1 1.5 %pack.1 = (bf16[2064,128]{1,0:T(8,128)(2,1)S(1)}, bf16[2064,128]{1,0:T(8,128)(2,1)S(1)}, bf16[592,128]{1,0:T(8,128)(2,1)S(1)}, f32[16,128]{1,0:T(8,128)S(1)}, bf...) custom-call(s32[1]{0:T(128)} %bitcast.tp, s32[1]{0:T(128)S(6)} %copy.13.lengths, s32[8]{0:T(128)} %owner.1, s32[64]{0:T(128)} %pos.1, ...), custom_call_target="tpu_custom_call" | custom-call | tf_op jit(solution)/shard_map/pack/pallas_call | solution.py:91
  5.7 3.3 %collective-permute-start.3 = (bf16[2064,128]{1,0:T(8,128)(2,1)S(1)}, bf16[2064,128]{1,0:T(8,128)(2,1)S(1)}, u32[]{:S(2)}, u32[]{:S(2)}) collective-permute-start(bf16[2064,128]{1,0:T(8,128)(2,1)S(1)} %get-tuple-element.49.kv0), channel_id=1, source_target_pairs={{0,16},{1,17},{2,18},{3,19},{4,20},{5,21},{6,22},{7,23},{8,24},{9,... | collective-permute-start | bytes 1585160 | tf_op jit(solution)/shard_map/ppermute | solution.py:51
  9.0 0.8 %collective-permute-start.5 = (bf16[2064,128]{1,0:T(8,128)(2,1)S(1)}, bf16[2064,128]{1,0:T(8,128)(2,1)S(1)}, u32[]{:S(2)}, u32[]{:S(2)}) collective-permute-start(bf16[2064,128]{1,0:T(8,128)(2,1)S(1)} %get-tuple-element.55), channel_id=1, source_target_pairs={{0,40},{1,41},{2,42},{3,43},{4,44},{5,45},{6,46},{7,47},{8,32},{9,... | collective-permute-start | bytes 1585160 | tf_op jit(solution)/shard_map/ppermute | solution.py:51
  9.8 1.3 %collective-permute-start.2 = (bf16[592,128]{1,0:T(8,128)(2,1)S(1)}, bf16[592,128]{1,0:T(8,128)(2,1)S(1)}, u32[]{:S(2)}, u32[]{:S(2)}) collective-permute-start(bf16[592,128]{1,0:T(8,128)(2,1)S(1)} %get-tuple-element.57.q0.q), channel_id=1, source_target_pairs={{0,64},{1,65},{2,66},{3,67},{4,68},{5,69},{6,70},{7,71},{8,72},{9,... | collective-permute-start | bytes 454664 | tf_op jit(solution)/shard_map/ppermute | solution.py:51
  11.1 1.9 %collective-permute-start.7 = (bf16[592,128]{1,0:T(8,128)(2,1)S(1)}, bf16[592,128]{1,0:T(8,128)(2,1)S(1)}, u32[]{:S(2)}, u32[]{:S(2)}) collective-permute-start(bf16[592,128]{1,0:T(8,128)(2,1)S(1)} %get-tuple-element.57.q0.q), channel_id=1, source_target_pairs={{0,192},{1,193},{2,194},{3,195},{4,196},{5,197},{6,198},{7,199},{8... | collective-permute-start | bytes 454664 | tf_op jit(solution)/shard_map/ppermute | solution.py:51
  13.0 1.5 %collective-permute-done.got = bf16[4,128,128]{2,1,0:T(8,128)(2,1)S(1)} collective-permute-done((bf16[4,128,128]{2,1,0:T(8,128)(2,1)S(1)}, bf16[4,128,128]{2,1,0:T(8,128)(2,1)S(1)}, u32[]{:S(2)}, u32[]{:S(2)}) %collective-permute-start) | collective-permute-done | bytes 131104 | tf_op jit(solution)/shard_map/ppermute | solution.py:51
  14.5 3.0 %collective-permute-start.6 = (bf16[592,128]{1,0:T(8,128)(2,1)S(1)}, bf16[592,128]{1,0:T(8,128)(2,1)S(1)}, u32[]{:S(2)}, u32[]{:S(2)}) collective-permute-start(bf16[592,128]{1,0:T(8,128)(2,1)S(1)} %get-tuple-element.57.q0.q), channel_id=1, source_target_pairs={{0,128},{1,129},{2,130},{3,131},{4,132},{5,133},{6,134},{7,135},{8... | collective-permute-start | bytes 454664 | tf_op jit(solution)/shard_map/ppermute | solution.py:51
  17.5 6.0 %collective-permute-start.1 = (bf16[2,128,128]{2,1,0:T(8,128)(2,1)S(1)}, bf16[2,128,128]{2,1,0:T(8,128)(2,1)S(1)}, u32[]{:S(2)}, u32[]{:S(2)}) collective-permute-start(bf16[2,128,128]{2,1,0:T(8,128)(2,1)S(1)} %get-tuple-element.47), channel_id=1, source_target_pairs={{0,6},{1,7},{2,4},{3,5},{4,2},{5,3},{6,0},{7,1},{8,14},{9,15},{10,... | collective-permute-start | bytes 196616 | tf_op jit(solution)/shard_map/ppermute | solution.py:51
  23.6 3.7 %cache_first.2 = (f32[1152,256]{1,0:T(8,128)S(1)}, f32[1152,128]{1,0:T(8,128)S(1)}) custom-call(s32[1]{0:T(128)} %bitcast.1.ctx, bf16[592,128]{1,0:T(8,128)(2,1)S(1)} %get-tuple-element.57.q0.q, bf16[592,128]{1,0:T(8,128)(2,1)S(1)} %collective-permute-done.2.q1, bf16[2064,128]{1,0:T(8,128)(2,1)S(1)} %get-tuple-element.49.kv0, ...), custom_call_target="tpu_custom_call" | custom-call | tf_op jit(solution)/shard_map/cache_first/pallas_call | solution.py:333
  27.3 1.3 %collective-permute-start.4 = (bf16[1,128,128]{2,1,0:T(8,128)(2,1)S(1)}, bf16[1,128,128]{2,1,0:T(8,128)(2,1)S(1)}, u32[]{:S(2)}, u32[]{:S(2)}) collective-permute-start(bf16[1,128,128]{2,1,0:T(8,128)(2,1)S(1)} %get-tuple-element.54), channel_id=1, source_target_pairs={{0,2},{1,3},{2,0},{3,1},{4,6},{5,7},{6,4},{7,5},{8,10},{9,11},{10,... | collective-permute-start | bytes 98312 | tf_op jit(solution)/shard_map/ppermute | solution.py:51
  28.6 3.9 %cache_first.3 = (f32[1152,256]{1,0:T(8,128)S(1)}, f32[1152,128]{1,0:T(8,128)S(1)}) custom-call(s32[1]{0:T(128)} %bitcast.1.ctx, bf16[592,128]{1,0:T(8,128)(2,1)S(1)} %collective-permute-done.6.q0, bf16[592,128]{1,0:T(8,128)(2,1)S(1)} %collective-permute-done.7.q1, bf16[2064,128]{1,0:T(8,128)(2,1)S(1)} %get-tuple-element.49.kv0, ...), custom_call_target="tpu_custom_call" | custom-call | tf_op jit(solution)/shard_map/cache_first/pallas_call | solution.py:333
  32.5 2.1 %collective-permute-start.9 = (bf16[2064,128]{1,0:T(8,128)(2,1)S(1)}, bf16[2064,128]{1,0:T(8,128)(2,1)S(1)}, u32[]{:S(2)}, u32[]{:S(2)}) collective-permute-start(bf16[2064,128]{1,0:T(8,128)(2,1)S(1)} %collective-permute-done.5.kv2), channel_id=1, source_target_pairs={{0,16},{1,17},{2,18},{3,19},{4,20},{5,21},{6,22},{7,23},{8,24},{9,... | collective-permute-start | bytes 1585160 | tf_op jit(solution)/shard_map/ppermute | solution.py:51
  34.7 0.8 %collective-permute-start.8 = (bf16[128,128]{1,0:T(8,128)(2,1)S(1)}, bf16[128,128]{1,0:T(8,128)(2,1)S(1)}, u32[]{:S(2)}, u32[]{:S(2)}) collective-permute-start(bf16[128,128]{1,0:T(8,128)(2,1)S(1)} %get-tuple-element.62), channel_id=1, source_target_pairs={{0,1},{1,0},{2,3},{3,2},{4,5},{5,4},{6,7},{7,6},{8,9},{9,8},{10,11... | collective-permute-start | bytes 98312 | tf_op jit(solution)/shard_map/ppermute | solution.py:51
  35.4 0.8 %collective-permute-done.9.kv3 = bf16[2064,128]{1,0:T(8,128)(2,1)S(1)} collective-permute-done((bf16[2064,128]{1,0:T(8,128)(2,1)S(1)}, bf16[2064,128]{1,0:T(8,128)(2,1)S(1)}, u32[]{:S(2)}, u32[]{:S(2)}) %collective-permute-start.9) | collective-permute-done | bytes 528416 | tf_op jit(solution)/shard_map/ppermute | solution.py:51
  36.2 2.0 %cache_second.2 = (bf16[592,128]{1,0:T(8,128)(2,1)S(1)}, bf16[592,128]{1,0:T(8,128)(2,1)S(1)}) custom-call(s32[1]{0:T(128)} %bitcast.1.ctx, bf16[592,128]{1,0:T(8,128)(2,1)S(1)} %get-tuple-element.57.q0.q, bf16[592,128]{1,0:T(8,128)(2,1)S(1)} %collective-permute-done.2.q1, bf16[2064,128]{1,0:T(8,128)(2,1)S(1)} %collective-permute-done.5.kv2, ...), custom_call_target="tpu_custom_call" | custom-call | tf_op jit(solution)/shard_map/cache_second/pallas_call | solution.py:333
  38.7 2.0 %cache_second.3 = (bf16[592,128]{1,0:T(8,128)(2,1)S(1)}, bf16[592,128]{1,0:T(8,128)(2,1)S(1)}) custom-call(s32[1]{0:T(128)} %bitcast.1.ctx, bf16[592,128]{1,0:T(8,128)(2,1)S(1)} %collective-permute-done.6.q0, bf16[592,128]{1,0:T(8,128)(2,1)S(1)} %collective-permute-done.7.q1, bf16[2064,128]{1,0:T(8,128)(2,1)S(1)} %collective-permute-done.5.kv2, ...), custom_call_target="tpu_custom_call" | custom-call | tf_op jit(solution)/shard_map/cache_second/pallas_call | solution.py:333
  40.8 1.9 %collective-permute-done.10.got = bf16[144,128]{1,0:T(8,128)(2,1)S(1)} collective-permute-done((bf16[144,128]{1,0:T(8,128)(2,1)S(1)}, bf16[144,128]{1,0:T(8,128)(2,1)S(1)}, u32[]{:S(2)}, u32[]{:S(2)}) %collective-permute-start.10) | collective-permute-done | bytes 36896 | tf_op jit(solution)/shard_map/ppermute | solution.py:51
  43.2 5.5 %collective-permute-start.12 = (bf16[880,128]{1,0:T(8,128)(2,1)S(1)}, bf16[880,128]{1,0:T(8,128)(2,1)S(1)}, u32[]{:S(2)}, u32[]{:S(2)}) collective-permute-start(bf16[880,128]{1,0:T(8,128)(2,1)S(1)} %get-tuple-element.74), channel_id=1, source_target_pairs={{0,128},{1,129},{2,130},{3,131},{4,132},{5,133},{6,134},{7,135},{8... | collective-permute-start | bytes 675848 | tf_op jit(solution)/shard_map/ppermute | solution.py:51
  48.7 9.8 %collective-permute-done.12.m2 = bf16[880,128]{1,0:T(8,128)(2,1)S(1)} collective-permute-done((bf16[880,128]{1,0:T(8,128)(2,1)S(1)}, bf16[880,128]{1,0:T(8,128)(2,1)S(1)}, u32[]{:S(2)}, u32[]{:S(2)}) %collective-permute-start.12) | collective-permute-done | bytes 225312 | tf_op jit(solution)/shard_map/ppermute | solution.py:51
  58.5 2.3 %collective-permute-done.13.m3 = bf16[880,128]{1,0:T(8,128)(2,1)S(1)} collective-permute-done((bf16[880,128]{1,0:T(8,128)(2,1)S(1)}, bf16[880,128]{1,0:T(8,128)(2,1)S(1)}, u32[]{:S(2)}, u32[]{:S(2)}) %collective-permute-start.13) | collective-permute-done | bytes 225312 | tf_op jit(solution)/shard_map/ppermute | solution.py:51
  60.9 1.9 %collective-permute-start.14 = (bf16[1152,128]{1,0:T(8,128)(2,1)S(1)}, bf16[1152,128]{1,0:T(8,128)(2,1)S(1)}, u32[]{:S(2)}, u32[]{:S(2)}) collective-permute-start(bf16[1152,128]{1,0:T(8,128)(2,1)S(1)} %near.1), channel_id=1, source_target_pairs={{0,16},{1,17},{2,18},{3,19},{4,20},{5,21},{6,22},{7,23},{8,24},{9,... | collective-permute-start | bytes 884744 | tf_op jit(solution)/shard_map/ppermute | solution.py:51
  62.8 1.6 %middle.1 = (bf16[8,1024]{1,0:T(8,128)(2,1)}, f32[512,128]{1,0:T(8,128)S(1)}, f32[512,128]{1,0:T(8,128)S(1)}) custom-call(bf16[592,128]{1,0:T(8,128)(2,1)S(1)} %get-tuple-element.57.q0.q, bf16[592,128]{1,0:T(8,128)(2,1)S(1)} %get-tuple-element.65.m0, bf16[880,128]{1,0:T(8,128)(2,1)S(1)} %collective-permute-done.11.m1, ...), custom_call_target="tpu_custom_call" | custom-call | tf_op jit(solution)/shard_map/middle/pallas_call | solution.py:435
  64.4 1.4 %final.1 = bf16[64,1024]{1,0:T(8,128)(2,1)} custom-call(bf16[592,128]{1,0:T(8,128)(2,1)S(1)} %get-tuple-element.57.q0.q, bf16[1152,128]{1,0:T(8,128)(2,1)S(1)} %collective-permute-done.14.far, f32[512,128]{1,0:T(8,128)S(1)} %get-tuple-element.80.value, f32[512,128]{1,0:T(8,128)S(1)} %get-tuple-element.78.level, f32[64,128]{1,0:T(8,128)S(1)} %get-tuple-element.77.pos), custom_call_target="tpu_custom_call" | custom-call | tf_op jit(solution)/shard_map/final/pallas_call | solution.py:435
  (20 shorter events, 1.2 us)
Async XLA Ops:
  5.7 17.9 %collective-permute-start.3 = (bf16[2064,128]{1,0:T(8,128)(2,1)S(1)}, bf16[2064,128]{1,0:T(8,128)(2,1)S(1)}, u32[]{:S(2)}, u32[]{:S(2)}) collective-permute-start(bf16[2064,128]{1,0:T(8,128)(2,1)S(1)} %get-tuple-element.49.kv0), channel_id=1, source_target_pairs={{0,16},{1,17},{2,18},{3,19},{4,20},{5,21},{6,22},{7,23},{8,24},{9,... | collective-permute-start | bytes 1585160 | tf_op jit(solution)/shard_map/ppermute | solution.py:51
  9.0 23.5 %collective-permute-start.5 = (bf16[2064,128]{1,0:T(8,128)(2,1)S(1)}, bf16[2064,128]{1,0:T(8,128)(2,1)S(1)}, u32[]{:S(2)}, u32[]{:S(2)}) collective-permute-start(bf16[2064,128]{1,0:T(8,128)(2,1)S(1)} %get-tuple-element.55), channel_id=1, source_target_pairs={{0,40},{1,41},{2,42},{3,43},{4,44},{5,45},{6,46},{7,47},{8,32},{9,... | collective-permute-start | bytes 1585160 | tf_op jit(solution)/shard_map/ppermute | solution.py:51
  9.8 4.7 %collective-permute-start = (bf16[4,128,128]{2,1,0:T(8,128)(2,1)S(1)}, bf16[4,128,128]{2,1,0:T(8,128)(2,1)S(1)}, u32[]{:S(2)}, u32[]{:S(2)}) collective-permute-start(bf16[4,128,128]{2,1,0:T(8,128)(2,1)S(1)} %get-tuple-element.42), channel_id=1, source_target_pairs={{0,8},{1,9},{2,10},{3,11},{4,12},{5,13},{6,14},{7,15},{8,0},{9,1},... | collective-permute-start | bytes 393224 | tf_op jit(solution)/shard_map/ppermute | solution.py:51
  9.8 7.7 %collective-permute-start.2 = (bf16[592,128]{1,0:T(8,128)(2,1)S(1)}, bf16[592,128]{1,0:T(8,128)(2,1)S(1)}, u32[]{:S(2)}, u32[]{:S(2)}) collective-permute-start(bf16[592,128]{1,0:T(8,128)(2,1)S(1)} %get-tuple-element.57.q0.q), channel_id=1, source_target_pairs={{0,64},{1,65},{2,66},{3,67},{4,68},{5,69},{6,70},{7,71},{8,72},{9,... | collective-permute-start | bytes 454664 | tf_op jit(solution)/shard_map/ppermute | solution.py:51
  11.1 17.5 %collective-permute-start.7 = (bf16[592,128]{1,0:T(8,128)(2,1)S(1)}, bf16[592,128]{1,0:T(8,128)(2,1)S(1)}, u32[]{:S(2)}, u32[]{:S(2)}) collective-permute-start(bf16[592,128]{1,0:T(8,128)(2,1)S(1)} %get-tuple-element.57.q0.q), channel_id=1, source_target_pairs={{0,192},{1,193},{2,194},{3,195},{4,196},{5,197},{6,198},{7,199},{8... | collective-permute-start | bytes 454664 | tf_op jit(solution)/shard_map/ppermute | solution.py:51
  14.5 14.1 %collective-permute-start.6 = (bf16[592,128]{1,0:T(8,128)(2,1)S(1)}, bf16[592,128]{1,0:T(8,128)(2,1)S(1)}, u32[]{:S(2)}, u32[]{:S(2)}) collective-permute-start(bf16[592,128]{1,0:T(8,128)(2,1)S(1)} %get-tuple-element.57.q0.q), channel_id=1, source_target_pairs={{0,128},{1,129},{2,130},{3,131},{4,132},{5,133},{6,134},{7,135},{8... | collective-permute-start | bytes 454664 | tf_op jit(solution)/shard_map/ppermute | solution.py:51
  17.5 9.8 %collective-permute-start.1 = (bf16[2,128,128]{2,1,0:T(8,128)(2,1)S(1)}, bf16[2,128,128]{2,1,0:T(8,128)(2,1)S(1)}, u32[]{:S(2)}, u32[]{:S(2)}) collective-permute-start(bf16[2,128,128]{2,1,0:T(8,128)(2,1)S(1)} %get-tuple-element.47), channel_id=1, source_target_pairs={{0,6},{1,7},{2,4},{3,5},{4,2},{5,3},{6,0},{7,1},{8,14},{9,15},{10,... | collective-permute-start | bytes 196616 | tf_op jit(solution)/shard_map/ppermute | solution.py:51
  27.3 5.2 %collective-permute-start.4 = (bf16[1,128,128]{2,1,0:T(8,128)(2,1)S(1)}, bf16[1,128,128]{2,1,0:T(8,128)(2,1)S(1)}, u32[]{:S(2)}, u32[]{:S(2)}) collective-permute-start(bf16[1,128,128]{2,1,0:T(8,128)(2,1)S(1)} %get-tuple-element.54), channel_id=1, source_target_pairs={{0,2},{1,3},{2,0},{3,1},{4,6},{5,7},{6,4},{7,5},{8,10},{9,11},{10,... | collective-permute-start | bytes 98312 | tf_op jit(solution)/shard_map/ppermute | solution.py:51
  32.5 3.7 %collective-permute-start.9 = (bf16[2064,128]{1,0:T(8,128)(2,1)S(1)}, bf16[2064,128]{1,0:T(8,128)(2,1)S(1)}, u32[]{:S(2)}, u32[]{:S(2)}) collective-permute-start(bf16[2064,128]{1,0:T(8,128)(2,1)S(1)} %collective-permute-done.5.kv2), channel_id=1, source_target_pairs={{0,16},{1,17},{2,18},{3,19},{4,20},{5,21},{6,22},{7,23},{8,24},{9,... | collective-permute-start | bytes 1585160 | tf_op jit(solution)/shard_map/ppermute | solution.py:51
  34.7 3.6 %collective-permute-start.8 = (bf16[128,128]{1,0:T(8,128)(2,1)S(1)}, bf16[128,128]{1,0:T(8,128)(2,1)S(1)}, u32[]{:S(2)}, u32[]{:S(2)}) collective-permute-start(bf16[128,128]{1,0:T(8,128)(2,1)S(1)} %get-tuple-element.62), channel_id=1, source_target_pairs={{0,1},{1,0},{2,3},{3,2},{4,5},{5,4},{6,7},{7,6},{8,9},{9,8},{10,11... | collective-permute-start | bytes 98312 | tf_op jit(solution)/shard_map/ppermute | solution.py:51
  38.3 4.4 %collective-permute-start.10 = (bf16[144,128]{1,0:T(8,128)(2,1)S(1)}, bf16[144,128]{1,0:T(8,128)(2,1)S(1)}, u32[]{:S(2)}, u32[]{:S(2)}) collective-permute-start(bf16[144,128]{1,0:T(8,128)(2,1)S(1)} %join.1.piece), channel_id=1, source_target_pairs={{0,32},{1,33},{2,34},{3,35},{4,36},{5,37},{6,38},{7,39},{8,40},{9,... | collective-permute-start | bytes 110600 | tf_op jit(solution)/shard_map/ppermute | solution.py:51
  42.7 6.0 %collective-permute-start.11 = (bf16[880,128]{1,0:T(8,128)(2,1)S(1)}, bf16[880,128]{1,0:T(8,128)(2,1)S(1)}, u32[]{:S(2)}, u32[]{:S(2)}) collective-permute-start(bf16[880,128]{1,0:T(8,128)(2,1)S(1)} %get-tuple-element.73), channel_id=1, source_target_pairs={{0,64},{1,65},{2,66},{3,67},{4,68},{5,69},{6,70},{7,71},{8,72},{9,... | collective-permute-start | bytes 675848 | tf_op jit(solution)/shard_map/ppermute | solution.py:51
  43.2 15.3 %collective-permute-start.12 = (bf16[880,128]{1,0:T(8,128)(2,1)S(1)}, bf16[880,128]{1,0:T(8,128)(2,1)S(1)}, u32[]{:S(2)}, u32[]{:S(2)}) collective-permute-start(bf16[880,128]{1,0:T(8,128)(2,1)S(1)} %get-tuple-element.74), channel_id=1, source_target_pairs={{0,128},{1,129},{2,130},{3,131},{4,132},{5,133},{6,134},{7,135},{8... | collective-permute-start | bytes 675848 | tf_op jit(solution)/shard_map/ppermute | solution.py:51
  48.7 12.2 %collective-permute-start.13 = (bf16[880,128]{1,0:T(8,128)(2,1)S(1)}, bf16[880,128]{1,0:T(8,128)(2,1)S(1)}, u32[]{:S(2)}, u32[]{:S(2)}) collective-permute-start(bf16[880,128]{1,0:T(8,128)(2,1)S(1)} %get-tuple-element.75), channel_id=1, source_target_pairs={{0,192},{1,193},{2,194},{3,195},{4,196},{5,197},{6,198},{7,199},{8... | collective-permute-start | bytes 675848 | tf_op jit(solution)/shard_map/ppermute | solution.py:51
  60.9 3.5 %collective-permute-start.14 = (bf16[1152,128]{1,0:T(8,128)(2,1)S(1)}, bf16[1152,128]{1,0:T(8,128)(2,1)S(1)}, u32[]{:S(2)}, u32[]{:S(2)}) collective-permute-start(bf16[1152,128]{1,0:T(8,128)(2,1)S(1)} %near.1), channel_id=1, source_target_pairs={{0,16},{1,17},{2,18},{3,19},{4,20},{5,21},{6,22},{7,23},{8,24},{9,... | collective-permute-start | bytes 884744 | tf_op jit(solution)/shard_map/ppermute | solution.py:51
where the time goes:
time: 65.3 us; the launch traced here: 65.7 us
  starting transfers between devices  28.8 us (44%)
  Pallas kernels  19.2 us (29%)
  waiting for transfers between devices  16.4 us (25%)
  between operations  1.39 us (2%)
    ppermute x15, starting transfers between devices, move(): return lax.ppermute(x, ('ctx', 'tp'), pairs)  28.8 us
    ppermute x15, waiting for transfers between devices, move(): return lax.ppermute(x, ('ctx', 'tp'), pairs)  16.4 us
    pallas_call x4, Pallas kernels, cache_call(): pl.pallas_call(kernel, in_specs=[pl.BlockSpec(memory_space=pltpu.SMEM)] +...  11.7 us
    pallas_call x2, Pallas kernels, far_call(): pl.pallas_call(kernel, in_specs=[pl.BlockSpec(memory_space=pltpu.SMEM)] *...  4.4 us
    pallas_call x2, Pallas kernels, last_call(): pl.pallas_call(kernel, in_specs=[whole] * len(arrays), out_specs=[whole]...  2.95 us
  transfers between devices with their start and end apart: 15, of which 5 were waited for; matrix products, arithmetic and copies ran while one was open for 0% of the time, Pallas kernels for 20%

commit v1 on v0

--- a/solution.py
+++ b/solution.py
@@ -51,6 +51,9 @@
     return lax.ppermute(x, ("ctx", "tp"), pairs)
 
 
+LIGHT = pl.CostEstimate(flops=1, bytes_accessed=1, transcendentals=0)
+
+
 def vmem(mib):
     return pltpu.CompilerParams(vmem_limit_bytes=mib * 1024 * 1024)
 
@@ -61,20 +64,10 @@
 PAIR = 2 * PIECE
 
 
-def project_kernel(tp, hidden, weight, send, keep, h, w, acc, sem_w, sem_h):
+def project_kernel(tp, h, w, send, keep, acc):
     side = tp[0] // 8
-    deep = hidden.shape[1] // PARTS
-    copy = pltpu.make_async_copy
-    copy_h = copy(hidden, h, sem_h)
-    copies = [
-        copy(weight.at[pl.ds(i * deep, deep)], w.at[pl.ds(i * deep, deep)], sem_w.at[i]) for i in range(PARTS)
-    ]
-    copy_h.start()
-    for x in copies:
-        x.start()
-    copy_h.wait()
+    deep = h.shape[1] // PARTS
     for i in range(PARTS):
-        copies[i].wait()
         part = slice(i * deep, (i + 1) * deep)
         product = jnp.dot(h[:, part], w[part, :], preferred_element_type=F32)
         acc[...] = product if i == 0 else acc[...] + product
@@ -96,21 +89,23 @@
         out_shape=[jax.ShapeDtypeStruct(shape, dtype) for shape, dtype in outs],
         scratch_shapes=scratch,
         compiler_params=vmem(12),
+        cost_estimate=LIGHT,
         name=name,
     )(*scalars, *[pltpu.with_memory_space_constraint(x, pltpu.HBM) for x in arrays])
 
 
 def project(tp, hidden, weight):
-    feats, width = weight.shape
     half = (4, 2 * ROWS, HD)
-    scratch = [
-        pltpu.VMEM((ROWS, feats), BF16),
-        pltpu.VMEM((feats, width), BF16),
-        pltpu.VMEM((ROWS, width), F32),
-        pltpu.SemaphoreType.DMA((PARTS,)),
-        pltpu.SemaphoreType.DMA,
-    ]
-    return far_call(project_kernel, (tp,), (hidden, weight), [(half, BF16), (half, F32)], scratch, "project")
+    whole = pl.BlockSpec(memory_space=pltpu.VMEM)
+    return pl.pallas_call(
+        project_kernel,
+        in_specs=[pl.BlockSpec(memory_space=pltpu.SMEM), whole, whole],
+        out_specs=[whole, whole],
+        out_shape=[jax.ShapeDtypeStruct(half, BF16), jax.ShapeDtypeStruct(half, F32)],
+        scratch_shapes=[pltpu.VMEM((ROWS, weight.shape[1]), F32)],
+        compiler_params=vmem(8),
+        name="project",
+    )(tp, hidden, weight)
 
 
 def pack_kernel(
@@ -198,6 +193,7 @@
         out_specs=[whole] * len(outs),
         out_shape=[jax.ShapeDtypeStruct(shape, dtype) for shape, dtype in outs],
         compiler_params=vmem(4),
+        cost_estimate=LIGHT,
         name=name,
     )(*scalars, *arrays)
 
@@ -228,18 +224,16 @@
     piece[2 * ROWS:PIECE, :] = line[...]
 
 
-def letters_kernel(piece, got, back1, back2, back3, out1, out2, out3):
-    for back, out in ((back1, out1), (back2, out2), (back3, out3)):
+def letters_kernel(piece, got, back, pair, letter):
+    for out in (pair, letter):
         out[0:PIECE, :] = piece[...]
         out[PIECE:PAIR, :] = got[...]
-        out[PAIR:PAIR + MSG, :] = back[...]
-
-
-def near_kernel(piece, got, m1, m2, m3, out):
-    out[0:PIECE, :] = piece[...]
-    out[PIECE:PAIR, :] = got[...]
-    for i, m in enumerate((m1, m2, m3)):
-        out[(i + 1) * PAIR:(i + 2) * PAIR, :] = m[0:PAIR, :]
+    letter[PAIR:PAIR + MSG, :] = back[...]
+
+
+def near_kernel(pair, g1, g2, m3, out):
+    for i, m in enumerate((pair, g1, g2, m3)):
+        out[i * PAIR:(i + 1) * PAIR, :] = m[0:PAIR, :]
 
 
 BLOCK = 192
@@ -337,6 +331,7 @@
         out_shape=[jax.ShapeDtypeStruct(shape, dtype) for shape, dtype in outs],
         scratch_shapes=[pltpu.VMEM(shape, F32) for shape in scratch],
         compiler_params=vmem(8),
+        cost_estimate=LIGHT,
         name=name,
     )(host, *arrays)
 
@@ -380,7 +375,7 @@
 
 
 def middle_kernel(q, m0, m1, m2, m3, near, own_kv, pos, out_d, value, level, keys, vals):
-    parts = ((m0, 0), (m1, PAIR), (m2, PAIR), (m3, PAIR))
+    parts = ((m0, 0), (m1, 0), (m2, 0), (m3, PAIR))
     where = lay_out(near, keys, vals)
     diagonal = lax.broadcasted_iota(jnp.int32, (HD, HD), 0) == lax.broadcasted_iota(jnp.int32, (HD, HD), 1)
 
@@ -439,6 +434,7 @@
         out_shape=[jax.ShapeDtypeStruct(shape, dtype) for shape, dtype in outs],
         scratch_shapes=[pltpu.VMEM((NEAR * ROWS, HD), BF16), pltpu.VMEM((NEAR * ROWS, 2 * HD), BF16)],
         compiler_params=vmem(8),
+        cost_estimate=LIGHT,
         name=name,
     )(*arrays)
 
@@ -452,7 +448,7 @@
     send, keep = project(tp, prompt_hidden, kv_weight)
     got = move(send, XLOW)
     kv_own, kv_give, q_own, own_kv, line, pos = pack(
-        tie(tp, send), cache_lengths, dec_owner, prompt_pos, cache_k, cache_v, prompt_q, dec_q, dec_k, dec_v
+        tp, cache_lengths, dec_owner, prompt_pos, cache_k, cache_v, prompt_q, dec_q, dec_k, dec_v
     )
     kv_adj = move(kv_give, XADJ)
     kv_core = move(kv_own, CORE)
@@ -461,31 +457,35 @@
 
     send, keep = halve(4, tp, keep, got)
     got = move(send, Z6)
-    q2 = move(tie(q_own, send), Y2)
-    groups = ((q_own, q1), (q2, q3))
+    q2 = move(q_own, Y2)
+    groups = ((q1, q2), (q_own, q3))
     state0 = cache_first(tie(host, send), groups[0], [kv_own, kv_core])
     got = tie(got, *state0)
     send, keep = halve(2, tp, keep, got)
     got = move(send, Z2)
-    state1 = cache_first(tie(host, send), groups[1], [kv_own, kv_core])
-    got = tie(got, kv_adj, *state1)
+    kv_diag = move(tie(kv_adj, send), CORE)
+    back0 = cache_second(tie(host, send), groups[0], [kv_adj, kv_diag], state0)
+    got = tie(got, *back0)
     half = (2 * ROWS, HD)
     send, total = glue(add_kernel, (), (keep, got), ((half, BF16), (half, F32)), "add")
     got = move(send, Z1)
-    kv_diag = move(tie(kv_adj, send), CORE)
-    back0 = cache_second(tie(host, send), groups[0], [kv_adj, kv_diag], state0)
-    got = tie(got, *back0)
+    m2 = move(tie(back0[1], send), Y2)
+    state1 = cache_first(tie(host, send), groups[1], [kv_own, kv_core])
+    got = tie(got, *state1)
     piece, = glue(join_kernel, (), (total, got, line), (((PIECE, HD), BF16),), "join")
     got = move(piece, XFAR)
+    m1 = move(tie(back0[0], piece), Y1)
     back1 = cache_second(tie(host, piece), groups[1], [kv_adj, kv_diag], state1)
-    got = tie(got, *back1)
-    letter = ((PAIR + MSG, HD), BF16)
-    letters = glue(letters_kernel, (), (piece, got, back0[1], *back1), (letter,) * 3, "letters")
-    parts = [move(x, pairs) for x, pairs in zip(letters, (Y1, Y2, Y3))]
-    near, = glue(near_kernel, (), (piece, got, *parts), (((4 * PAIR, HD), BF16),), "near")
+    got = tie(got, m1, m2, *back1)
+    mine, back3 = back1
+    pair, letter = glue(
+        letters_kernel, (), (piece, got, back3), (((PAIR, HD), BF16), ((PAIR + MSG, HD), BF16)), "letters"
+    )
+    g2, g1, m3 = move(pair, Y2), move(pair, Y1), move(letter, Y3)
+    near, = glue(near_kernel, (), (pair, g1, g2, m3), (((4 * PAIR, HD), BF16),), "near")
     far = move(near, CORE)
     out_d, value, level = last_call(
-        middle_kernel, (q_own, back0[0], *parts, near, own_kv, pos),
+        middle_kernel, (q_own, mine, m1, m2, m3, near, own_kv, pos),
         [((DROWS, HEADS * HD), BF16), ((PR, HD), F32), ((PR, HD), F32)], "middle",
     )
     far = tie(far, level)

time: 65.3 us -> 59.5 us (0.911)
  waiting for transfers between devices: 16.4 us -> 4.79 us
  starting transfers between devices: 28.8 us -> 32.1 us
  Pallas kernels: 19.2 us -> 20.9 us
    ppermute x15 -> x17, waiting for transfers between devices: 16.4 us -> 4.79 us  [move(): return lax.ppermute(x, ('ctx', 'tp'), pairs)]
    pallas_call x4, Pallas kernels: 11.7 us -> 15.2 us  [cache_call(): pl.pallas_call(kernel, in_specs=[pl.BlockSpec(memory_space=pltpu.SMEM)] +...]
    ppermute x15 -> x17, starting transfers between devices: 28.8 us -> 32.1 us  [move(): return lax.ppermute(x, ('ctx', 'tp'), pairs)]
    pallas_call x2 -> x1, Pallas kernels: 4.4 us -> 1.67 us  [far_call(): pl.pallas_call(kernel, in_specs=[pl.BlockSpec(memory_space=pltpu.SMEM)] *...]
    pallas_call x0 -> x1, Pallas kernels: none -> 0.91 us  [project(): pl.pallas_call(project_kernel, in_specs=[pl.BlockSpec(memory_space=pltpu....]
  transfers between devices with their start and end apart: 15 -> 17, of which waited for: 5 -> 4; matrix products, arithmetic and copies ran while one was open for 0% -> 0% of each run, Pallas kernels for 20% -> 30%
where the time goes in v1:
time: 59.5 us; the launch traced here: 59.3 us
  starting transfers between devices  32.1 us (54%)
  Pallas kernels  20.9 us (35%)
  waiting for transfers between devices  4.79 us (8%)
  between operations  1.44 us (2%)
    ppermute x17, starting transfers between devices, move(): return lax.ppermute(x, ('ctx', 'tp'), pairs)  32.1 us
    pallas_call x4, Pallas kernels, cache_call(): pl.pallas_call(kernel, in_specs=[pl.BlockSpec(memory_space=pltpu.SMEM)] +...  15.2 us
    ppermute x17, waiting for transfers between devices, move(): return lax.ppermute(x, ('ctx', 'tp'), pairs)  4.79 us
    pallas_call x2, Pallas kernels, last_call(): pl.pallas_call(kernel, in_specs=[whole] * len(arrays), out_specs=[whole]...  2.97 us
    pallas_call x1, Pallas kernels, far_call(): pl.pallas_call(kernel, in_specs=[pl.BlockSpec(memory_space=pltpu.SMEM)] *...  1.67 us
  transfers between devices with their start and end apart: 17, of which 4 were waited for; matrix products, arithmetic and copies ran while one was open for 0% of the time, Pallas kernels for 30%

profile of v1, /device:TPU:1, one launch (start us, length us, event | category | flops | bytes accessed | tf_op | source)
XLA Modules:
  0.0 59.3 jit_solution(2576574701401621659)
XLA Ops:
  1.3 1.7 %pack.1 = (bf16[2064,128]{1,0:T(8,128)(2,1)S(1)}, bf16[2064,128]{1,0:T(8,128)(2,1)S(1)}, bf16[592,128]{1,0:T(8,128)(2,1)S(1)}, f32[16,128]{1,0:T(8,128)S(1)}, bf...) custom-call(s32[1]{0:T(128)} %bitcast.tp, s32[1]{0:T(128)S(6)} %copy.13.lengths, s32[8]{0:T(128)} %owner.1, s32[64]{0:T(128)} %pos.1, ...), custom_call_target="tpu_custom_call" | custom-call | flops 1 | bytes 1 | tf_op jit(solution)/shard_map/pack/pallas_call | solution.py:84
  3.0 3.3 %collective-permute-start.4 = (bf16[2064,128]{1,0:T(8,128)(2,1)S(1)}, bf16[2064,128]{1,0:T(8,128)(2,1)S(1)}, u32[]{:S(2)}, u32[]{:S(2)}) collective-permute-start(bf16[2064,128]{1,0:T(8,128)(2,1)S(1)} %get-tuple-element.47.kv0), channel_id=1, source_target_pairs={{0,16},{1,17},{2,18},{3,19},{4,20},{5,21},{6,22},{7,23},{8,24},{9,... | collective-permute-start | bytes 1585160 | tf_op jit(solution)/shard_map/ppermute | solution.py:51
  6.3 0.8 %collective-permute-start.6 = (bf16[2064,128]{1,0:T(8,128)(2,1)S(1)}, bf16[2064,128]{1,0:T(8,128)(2,1)S(1)}, u32[]{:S(2)}, u32[]{:S(2)}) collective-permute-start(bf16[2064,128]{1,0:T(8,128)(2,1)S(1)} %get-tuple-element.54), channel_id=1, source_target_pairs={{0,40},{1,41},{2,42},{3,43},{4,44},{5,45},{6,46},{7,47},{8,32},{9,... | collective-permute-start | bytes 1585160 | tf_op jit(solution)/shard_map/ppermute | solution.py:51
  7.1 0.9 %project.1 = (bf16[4,128,128]{2,1,0:T(8,128)(2,1)S(1)}, f32[4,128,128]{2,1,0:T(8,128)S(1)}) custom-call(s32[1]{0:T(128)} %bitcast.tp, bf16[64,1024]{1,0:T(8,128)(2,1)S(1)} %copy-done.1, bf16[1024,2048]{1,0:T(8,128)(2,1)S(1)} %copy-done), custom_call_target="tpu_custom_call" | custom-call | tf_op jit(solution)/shard_map/project/pallas_call | solution.py:100
  8.1 1.4 %collective-permute-start.2 = (bf16[592,128]{1,0:T(8,128)(2,1)S(1)}, bf16[592,128]{1,0:T(8,128)(2,1)S(1)}, u32[]{:S(2)}, u32[]{:S(2)}) collective-permute-start(bf16[592,128]{1,0:T(8,128)(2,1)S(1)} %get-tuple-element.41.q0.q), channel_id=1, source_target_pairs={{0,64},{1,65},{2,66},{3,67},{4,68},{5,69},{6,70},{7,71},{8,72},{9,... | collective-permute-start | bytes 454664 | tf_op jit(solution)/shard_map/ppermute | solution.py:51
  9.5 2.6 %collective-permute-start.3 = (bf16[592,128]{1,0:T(8,128)(2,1)S(1)}, bf16[592,128]{1,0:T(8,128)(2,1)S(1)}, u32[]{:S(2)}, u32[]{:S(2)}) collective-permute-start(bf16[592,128]{1,0:T(8,128)(2,1)S(1)} %get-tuple-element.41.q0.q), channel_id=1, source_target_pairs={{0,128},{1,129},{2,130},{3,131},{4,132},{5,133},{6,134},{7,135},{8... | collective-permute-start | bytes 454664 | tf_op jit(solution)/shard_map/ppermute | solution.py:51
  12.1 0.7 %collective-permute-done.got = bf16[4,128,128]{2,1,0:T(8,128)(2,1)S(1)} collective-permute-done((bf16[4,128,128]{2,1,0:T(8,128)(2,1)S(1)}, bf16[4,128,128]{2,1,0:T(8,128)(2,1)S(1)}, u32[]{:S(2)}, u32[]{:S(2)}) %collective-permute-start) | collective-permute-done | bytes 131104 | tf_op jit(solution)/shard_map/ppermute | solution.py:51
  12.8 6.1 %collective-permute-start.1 = (bf16[2,128,128]{2,1,0:T(8,128)(2,1)S(1)}, bf16[2,128,128]{2,1,0:T(8,128)(2,1)S(1)}, u32[]{:S(2)}, u32[]{:S(2)}) collective-permute-start(bf16[2,128,128]{2,1,0:T(8,128)(2,1)S(1)} %get-tuple-element.45), channel_id=1, source_target_pairs={{0,6},{1,7},{2,4},{3,5},{4,2},{5,3},{6,0},{7,1},{8,14},{9,15},{10,... | collective-permute-start | bytes 196616 | tf_op jit(solution)/shard_map/ppermute | solution.py:51
  18.9 4.0 %cache_first.2 = (f32[1152,256]{1,0:T(8,128)S(1)}, f32[1152,128]{1,0:T(8,128)S(1)}) custom-call(s32[1]{0:T(128)} %bitcast.1.ctx, bf16[592,128]{1,0:T(8,128)(2,1)S(1)} %collective-permute-done.2.q0, bf16[592,128]{1,0:T(8,128)(2,1)S(1)} %collective-permute-done.3.q1, bf16[2064,128]{1,0:T(8,128)(2,1)S(1)} %get-tuple-element.47.kv0, ...), custom_call_target="tpu_custom_call" | custom-call | flops 1 | bytes 1 | tf_op jit(solution)/shard_map/cache_first/pallas_call | solution.py:327
  23.0 1.6 %collective-permute-start.7 = (bf16[2064,128]{1,0:T(8,128)(2,1)S(1)}, bf16[2064,128]{1,0:T(8,128)(2,1)S(1)}, u32[]{:S(2)}, u32[]{:S(2)}) collective-permute-start(bf16[2064,128]{1,0:T(8,128)(2,1)S(1)} %collective-permute-done.6.kv2), channel_id=1, source_target_pairs={{0,16},{1,17},{2,18},{3,19},{4,20},{5,21},{6,22},{7,23},{8,24},{9,... | collective-permute-start | bytes 1585160 | tf_op jit(solution)/shard_map/ppermute | solution.py:51
  24.6 1.6 %collective-permute-start.9 = (bf16[592,128]{1,0:T(8,128)(2,1)S(1)}, bf16[592,128]{1,0:T(8,128)(2,1)S(1)}, u32[]{:S(2)}, u32[]{:S(2)}) collective-permute-start(bf16[592,128]{1,0:T(8,128)(2,1)S(1)} %get-tuple-element.41.q0.q), channel_id=1, source_target_pairs={{0,192},{1,193},{2,194},{3,195},{4,196},{5,197},{6,198},{7,199},{8... | collective-permute-start | bytes 454664 | tf_op jit(solution)/shard_map/ppermute | solution.py:51
  26.2 1.2 %collective-permute-start.5 = (bf16[1,128,128]{2,1,0:T(8,128)(2,1)S(1)}, bf16[1,128,128]{2,1,0:T(8,128)(2,1)S(1)}, u32[]{:S(2)}, u32[]{:S(2)}) collective-permute-start(bf16[1,128,128]{2,1,0:T(8,128)(2,1)S(1)} %get-tuple-element.52), channel_id=1, source_target_pairs={{0,2},{1,3},{2,0},{3,1},{4,6},{5,7},{6,4},{7,5},{8,10},{9,11},{10,... | collective-permute-start | bytes 98312 | tf_op jit(solution)/shard_map/ppermute | solution.py:51
  27.4 3.7 %cache_second.2 = (bf16[592,128]{1,0:T(8,128)(2,1)S(1)}, bf16[592,128]{1,0:T(8,128)(2,1)S(1)}) custom-call(s32[1]{0:T(128)} %bitcast.1.ctx, bf16[592,128]{1,0:T(8,128)(2,1)S(1)} %collective-permute-done.2.q0, bf16[592,128]{1,0:T(8,128)(2,1)S(1)} %collective-permute-done.3.q1, bf16[2064,128]{1,0:T(8,128)(2,1)S(1)} %collective-permute-done.6.kv2, ...), custom_call_target="tpu_custom_call" | custom-call | flops 1 | bytes 1 | tf_op jit(solution)/shard_map/cache_second/pallas_call | solution.py:327
  31.2 1.7 %collective-permute-start.8 = (bf16[128,128]{1,0:T(8,128)(2,1)S(1)}, bf16[128,128]{1,0:T(8,128)(2,1)S(1)}, u32[]{:S(2)}, u32[]{:S(2)}) collective-permute-start(bf16[128,128]{1,0:T(8,128)(2,1)S(1)} %get-tuple-element.60), channel_id=1, source_target_pairs={{0,1},{1,0},{2,3},{3,2},{4,5},{5,4},{6,7},{7,6},{8,9},{9,8},{10,11... | collective-permute-start | bytes 98312 | tf_op jit(solution)/shard_map/ppermute | solution.py:51
  32.9 2.5 %collective-permute-start.12 = (bf16[592,128]{1,0:T(8,128)(2,1)S(1)}, bf16[592,128]{1,0:T(8,128)(2,1)S(1)}, u32[]{:S(2)}, u32[]{:S(2)}) collective-permute-start(bf16[592,128]{1,0:T(8,128)(2,1)S(1)} %get-tuple-element.67), channel_id=1, source_target_pairs={{0,128},{1,129},{2,130},{3,131},{4,132},{5,133},{6,134},{7,135},{8... | collective-permute-start | bytes 454664 | tf_op jit(solution)/shard_map/ppermute | solution.py:51
  35.4 3.9 %cache_first.3 = (f32[1152,256]{1,0:T(8,128)S(1)}, f32[1152,128]{1,0:T(8,128)S(1)}) custom-call(s32[1]{0:T(128)} %bitcast.1.ctx, bf16[592,128]{1,0:T(8,128)(2,1)S(1)} %get-tuple-element.41.q0.q, bf16[592,128]{1,0:T(8,128)(2,1)S(1)} %collective-permute-done.9.q1, bf16[2064,128]{1,0:T(8,128)(2,1)S(1)} %get-tuple-element.47.kv0, ...), custom_call_target="tpu_custom_call" | custom-call | flops 1 | bytes 1 | tf_op jit(solution)/shard_map/cache_first/pallas_call | solution.py:327
  39.4 1.7 %collective-permute-start.11 = (bf16[592,128]{1,0:T(8,128)(2,1)S(1)}, bf16[592,128]{1,0:T(8,128)(2,1)S(1)}, u32[]{:S(2)}, u32[]{:S(2)}) collective-permute-start(bf16[592,128]{1,0:T(8,128)(2,1)S(1)} %get-tuple-element.66), channel_id=1, source_target_pairs={{0,64},{1,65},{2,66},{3,67},{4,68},{5,69},{6,70},{7,71},{8,72},{9,... | collective-permute-start | bytes 454664 | tf_op jit(solution)/shard_map/ppermute | solution.py:51
  41.0 3.6 %cache_second.3 = (bf16[592,128]{1,0:T(8,128)(2,1)S(1)}, bf16[592,128]{1,0:T(8,128)(2,1)S(1)}) custom-call(s32[1]{0:T(128)} %bitcast.1.ctx, bf16[592,128]{1,0:T(8,128)(2,1)S(1)} %get-tuple-element.41.q0.q, bf16[592,128]{1,0:T(8,128)(2,1)S(1)} %collective-permute-done.9.q1, bf16[2064,128]{1,0:T(8,128)(2,1)S(1)} %collective-permute-done.6.kv2, ...), custom_call_target="tpu_custom_call" | custom-call | flops 1 | bytes 1 | tf_op jit(solution)/shard_map/cache_second/pallas_call | solution.py:327
  44.6 0.7 %collective-permute-done.10.got = bf16[144,128]{1,0:T(8,128)(2,1)S(1)} collective-permute-done((bf16[144,128]{1,0:T(8,128)(2,1)S(1)}, bf16[144,128]{1,0:T(8,128)(2,1)S(1)}, u32[]{:S(2)}, u32[]{:S(2)}) %collective-permute-start.10) | collective-permute-done | bytes 36896 | tf_op jit(solution)/shard_map/ppermute | solution.py:51
  45.7 3.7 %collective-permute-start.14 = (bf16[288,128]{1,0:T(8,128)(2,1)S(1)}, bf16[288,128]{1,0:T(8,128)(2,1)S(1)}, u32[]{:S(2)}, u32[]{:S(2)}) collective-permute-start(bf16[288,128]{1,0:T(8,128)(2,1)S(1)} %get-tuple-element.72.pair), channel_id=1, source_target_pairs={{0,128},{1,129},{2,130},{3,131},{4,132},{5,133},{6,134},{7,135},{8... | collective-permute-start | bytes 221192 | tf_op jit(solution)/shard_map/ppermute | solution.py:51
  49.4 2.6 %collective-permute-done.14.g2 = bf16[288,128]{1,0:T(8,128)(2,1)S(1)} collective-permute-done((bf16[288,128]{1,0:T(8,128)(2,1)S(1)}, bf16[288,128]{1,0:T(8,128)(2,1)S(1)}, u32[]{:S(2)}, u32[]{:S(2)}) %collective-permute-start.14) | collective-permute-done | bytes 73760 | tf_op jit(solution)/shard_map/ppermute | solution.py:51
  52.7 3.6 %collective-permute-start.16 = (bf16[1152,128]{1,0:T(8,128)(2,1)S(1)}, bf16[1152,128]{1,0:T(8,128)(2,1)S(1)}, u32[]{:S(2)}, u32[]{:S(2)}) collective-permute-start(bf16[1152,128]{1,0:T(8,128)(2,1)S(1)} %near.1), channel_id=1, source_target_pairs={{0,16},{1,17},{2,18},{3,19},{4,20},{5,21},{6,22},{7,23},{8,24},{9,... | collective-permute-start | bytes 884744 | tf_op jit(solution)/shard_map/ppermute | solution.py:51
  56.3 1.6 %middle.1 = (bf16[8,1024]{1,0:T(8,128)(2,1)}, f32[512,128]{1,0:T(8,128)S(1)}, f32[512,128]{1,0:T(8,128)S(1)}) custom-call(bf16[592,128]{1,0:T(8,128)(2,1)S(1)} %get-tuple-element.41.q0.q, bf16[592,128]{1,0:T(8,128)(2,1)S(1)} %get-tuple-element.69.m0, bf16[592,128]{1,0:T(8,128)(2,1)S(1)} %collective-permute-done.11.m1, ...), custom_call_target="tpu_custom_call" | custom-call | flops 1 | bytes 1 | tf_op jit(solution)/shard_map/middle/pallas_call | solution.py:430
  57.9 1.4 %final.1 = bf16[64,1024]{1,0:T(8,128)(2,1)} custom-call(bf16[592,128]{1,0:T(8,128)(2,1)S(1)} %get-tuple-element.41.q0.q, bf16[1152,128]{1,0:T(8,128)(2,1)S(1)} %collective-permute-done.16.far, f32[512,128]{1,0:T(8,128)S(1)} %get-tuple-element.78.value, f32[512,128]{1,0:T(8,128)S(1)} %get-tuple-element.76.level, f32[64,128]{1,0:T(8,128)S(1)} %get-tuple-element.75.pos), custom_call_target="tpu_custom_call" | custom-call | flops 1 | bytes 1 | tf_op jit(solution)/shard_map/final/pallas_call | solution.py:430
  (28 shorter events, 1.2 us)
Async XLA Ops:
  1.3 5.8 %copy-start = (bf16[1024,2048]{1,0:T(8,128)(2,1)S(1)}, bf16[1024,2048]{1,0:T(8,128)(2,1)}, u32[]{:S(2)}) copy-start(bf16[1024,2048]{1,0:T(8,128)(2,1)} %w.1) | copy-start | bytes 12582916
  1.3 5.8 %copy-start.1 = (bf16[64,1024]{1,0:T(8,128)(2,1)S(1)}, bf16[64,1024]{1,0:T(8,128)(2,1)}, u32[]{:S(2)}) copy-start(bf16[64,1024]{1,0:T(8,128)(2,1)} %h.1) | copy-start | bytes 393220
  3.0 16.0 %collective-permute-start.4 = (bf16[2064,128]{1,0:T(8,128)(2,1)S(1)}, bf16[2064,128]{1,0:T(8,128)(2,1)S(1)}, u32[]{:S(2)}, u32[]{:S(2)}) collective-permute-start(bf16[2064,128]{1,0:T(8,128)(2,1)S(1)} %get-tuple-element.47.kv0), channel_id=1, source_target_pairs={{0,16},{1,17},{2,18},{3,19},{4,20},{5,21},{6,22},{7,23},{8,24},{9,... | collective-permute-start | bytes 1585160 | tf_op jit(solution)/shard_map/ppermute | solution.py:51
  6.3 16.7 %collective-permute-start.6 = (bf16[2064,128]{1,0:T(8,128)(2,1)S(1)}, bf16[2064,128]{1,0:T(8,128)(2,1)S(1)}, u32[]{:S(2)}, u32[]{:S(2)}) collective-permute-start(bf16[2064,128]{1,0:T(8,128)(2,1)S(1)} %get-tuple-element.54), channel_id=1, source_target_pairs={{0,40},{1,41},{2,42},{3,43},{4,44},{5,45},{6,46},{7,47},{8,32},{9,... | collective-permute-start | bytes 1585160 | tf_op jit(solution)/shard_map/ppermute | solution.py:51
  8.0 4.8 %collective-permute-start = (bf16[4,128,128]{2,1,0:T(8,128)(2,1)S(1)}, bf16[4,128,128]{2,1,0:T(8,128)(2,1)S(1)}, u32[]{:S(2)}, u32[]{:S(2)}) collective-permute-start(bf16[4,128,128]{2,1,0:T(8,128)(2,1)S(1)} %get-tuple-element.43), channel_id=1, source_target_pairs={{0,8},{1,9},{2,10},{3,11},{4,12},{5,13},{6,14},{7,15},{8,0},{9,1},... | collective-permute-start | bytes 393224 | tf_op jit(solution)/shard_map/ppermute | solution.py:51
  8.1 10.8 %collective-permute-start.2 = (bf16[592,128]{1,0:T(8,128)(2,1)S(1)}, bf16[592,128]{1,0:T(8,128)(2,1)S(1)}, u32[]{:S(2)}, u32[]{:S(2)}) collective-permute-start(bf16[592,128]{1,0:T(8,128)(2,1)S(1)} %get-tuple-element.41.q0.q), channel_id=1, source_target_pairs={{0,64},{1,65},{2,66},{3,67},{4,68},{5,69},{6,70},{7,71},{8,72},{9,... | collective-permute-start | bytes 454664 | tf_op jit(solution)/shard_map/ppermute | solution.py:51
  9.5 9.5 %collective-permute-start.3 = (bf16[592,128]{1,0:T(8,128)(2,1)S(1)}, bf16[592,128]{1,0:T(8,128)(2,1)S(1)}, u32[]{:S(2)}, u32[]{:S(2)}) collective-permute-start(bf16[592,128]{1,0:T(8,128)(2,1)S(1)} %get-tuple-element.41.q0.q), channel_id=1, source_target_pairs={{0,128},{1,129},{2,130},{3,131},{4,132},{5,133},{6,134},{7,135},{8... | collective-permute-start | bytes 454664 | tf_op jit(solution)/shard_map/ppermute | solution.py:51
  12.8 10.1 %collective-permute-start.1 = (bf16[2,128,128]{2,1,0:T(8,128)(2,1)S(1)}, bf16[2,128,128]{2,1,0:T(8,128)(2,1)S(1)}, u32[]{:S(2)}, u32[]{:S(2)}) collective-permute-start(bf16[2,128,128]{2,1,0:T(8,128)(2,1)S(1)} %get-tuple-element.45), channel_id=1, source_target_pairs={{0,6},{1,7},{2,4},{3,5},{4,2},{5,3},{6,0},{7,1},{8,14},{9,15},{10,... | collective-permute-start | bytes 196616 | tf_op jit(solution)/shard_map/ppermute | solution.py:51
  23.0 4.4 %collective-permute-start.7 = (bf16[2064,128]{1,0:T(8,128)(2,1)S(1)}, bf16[2064,128]{1,0:T(8,128)(2,1)S(1)}, u32[]{:S(2)}, u32[]{:S(2)}) collective-permute-start(bf16[2064,128]{1,0:T(8,128)(2,1)S(1)} %collective-permute-done.6.kv2), channel_id=1, source_target_pairs={{0,16},{1,17},{2,18},{3,19},{4,20},{5,21},{6,22},{7,23},{8,24},{9,... | collective-permute-start | bytes 1585160 | tf_op jit(solution)/shard_map/ppermute | solution.py:51
  24.6 10.8 %collective-permute-start.9 = (bf16[592,128]{1,0:T(8,128)(2,1)S(1)}, bf16[592,128]{1,0:T(8,128)(2,1)S(1)}, u32[]{:S(2)}, u32[]{:S(2)}) collective-permute-start(bf16[592,128]{1,0:T(8,128)(2,1)S(1)} %get-tuple-element.41.q0.q), channel_id=1, source_target_pairs={{0,192},{1,193},{2,194},{3,195},{4,196},{5,197},{6,198},{7,199},{8... | collective-permute-start | bytes 454664 | tf_op jit(solution)/shard_map/ppermute | solution.py:51
  26.2 4.9 %collective-permute-start.5 = (bf16[1,128,128]{2,1,0:T(8,128)(2,1)S(1)}, bf16[1,128,128]{2,1,0:T(8,128)(2,1)S(1)}, u32[]{:S(2)}, u32[]{:S(2)}) collective-permute-start(bf16[1,128,128]{2,1,0:T(8,128)(2,1)S(1)} %get-tuple-element.52), channel_id=1, source_target_pairs={{0,2},{1,3},{2,0},{3,1},{4,6},{5,7},{6,4},{7,5},{8,10},{9,11},{10,... | collective-permute-start | bytes 98312 | tf_op jit(solution)/shard_map/ppermute | solution.py:51
  31.2 8.2 %collective-permute-start.8 = (bf16[128,128]{1,0:T(8,128)(2,1)S(1)}, bf16[128,128]{1,0:T(8,128)(2,1)S(1)}, u32[]{:S(2)}, u32[]{:S(2)}) collective-permute-start(bf16[128,128]{1,0:T(8,128)(2,1)S(1)} %get-tuple-element.60), channel_id=1, source_target_pairs={{0,1},{1,0},{2,3},{3,2},{4,5},{5,4},{6,7},{7,6},{8,9},{9,8},{10,11... | collective-permute-start | bytes 98312 | tf_op jit(solution)/shard_map/ppermute | solution.py:51
  32.9 12.5 %collective-permute-start.12 = (bf16[592,128]{1,0:T(8,128)(2,1)S(1)}, bf16[592,128]{1,0:T(8,128)(2,1)S(1)}, u32[]{:S(2)}, u32[]{:S(2)}) collective-permute-start(bf16[592,128]{1,0:T(8,128)(2,1)S(1)} %get-tuple-element.67), channel_id=1, source_target_pairs={{0,128},{1,129},{2,130},{3,131},{4,132},{5,133},{6,134},{7,135},{8... | collective-permute-start | bytes 454664 | tf_op jit(solution)/shard_map/ppermute | solution.py:51
  39.4 6.0 %collective-permute-start.11 = (bf16[592,128]{1,0:T(8,128)(2,1)S(1)}, bf16[592,128]{1,0:T(8,128)(2,1)S(1)}, u32[]{:S(2)}, u32[]{:S(2)}) collective-permute-start(bf16[592,128]{1,0:T(8,128)(2,1)S(1)} %get-tuple-element.66), channel_id=1, source_target_pairs={{0,64},{1,65},{2,66},{3,67},{4,68},{5,69},{6,70},{7,71},{8,72},{9,... | collective-permute-start | bytes 454664 | tf_op jit(solution)/shard_map/ppermute | solution.py:51
  41.0 4.3 %collective-permute-start.10 = (bf16[144,128]{1,0:T(8,128)(2,1)S(1)}, bf16[144,128]{1,0:T(8,128)(2,1)S(1)}, u32[]{:S(2)}, u32[]{:S(2)}) collective-permute-start(bf16[144,128]{1,0:T(8,128)(2,1)S(1)} %join.1.piece), channel_id=1, source_target_pairs={{0,32},{1,33},{2,34},{3,35},{4,36},{5,37},{6,38},{7,39},{8,40},{9,... | collective-permute-start | bytes 110600 | tf_op jit(solution)/shard_map/ppermute | solution.py:51
  45.4 7.3 %collective-permute-start.15 = (bf16[880,128]{1,0:T(8,128)(2,1)S(1)}, bf16[880,128]{1,0:T(8,128)(2,1)S(1)}, u32[]{:S(2)}, u32[]{:S(2)}) collective-permute-start(bf16[880,128]{1,0:T(8,128)(2,1)S(1)} %get-tuple-element.73), channel_id=1, source_target_pairs={{0,192},{1,193},{2,194},{3,195},{4,196},{5,197},{6,198},{7,199},{8... | collective-permute-start | bytes 675848 | tf_op jit(solution)/shard_map/ppermute | solution.py:51
  45.5 3.8 %collective-permute-start.13 = (bf16[288,128]{1,0:T(8,128)(2,1)S(1)}, bf16[288,128]{1,0:T(8,128)(2,1)S(1)}, u32[]{:S(2)}, u32[]{:S(2)}) collective-permute-start(bf16[288,128]{1,0:T(8,128)(2,1)S(1)} %get-tuple-element.72.pair), channel_id=1, source_target_pairs={{0,64},{1,65},{2,66},{3,67},{4,68},{5,69},{6,70},{7,71},{8,72},{9,... | collective-permute-start | bytes 221192 | tf_op jit(solution)/shard_map/ppermute | solution.py:51
  45.7 6.3 %collective-permute-start.14 = (bf16[288,128]{1,0:T(8,128)(2,1)S(1)}, bf16[288,128]{1,0:T(8,128)(2,1)S(1)}, u32[]{:S(2)}, u32[]{:S(2)}) collective-permute-start(bf16[288,128]{1,0:T(8,128)(2,1)S(1)} %get-tuple-element.72.pair), channel_id=1, source_target_pairs={{0,128},{1,129},{2,130},{3,131},{4,132},{5,133},{6,134},{7,135},{8... | collective-permute-start | bytes 221192 | tf_op jit(solution)/shard_map/ppermute | solution.py:51
  52.7 5.2 %collective-permute-start.16 = (bf16[1152,128]{1,0:T(8,128)(2,1)S(1)}, bf16[1152,128]{1,0:T(8,128)(2,1)S(1)}, u32[]{:S(2)}, u32[]{:S(2)}) collective-permute-start(bf16[1152,128]{1,0:T(8,128)(2,1)S(1)} %near.1), channel_id=1, source_target_pairs={{0,16},{1,17},{2,18},{3,19},{4,20},{5,21},{6,22},{7,23},{8,24},{9,... | collective-permute-start | bytes 884744 | tf_op jit(solution)/shard_map/ppermute | solution.py:51

commit v2 on v1

--- a/solution.py
+++ b/solution.py
@@ -224,19 +224,18 @@
     piece[2 * ROWS:PIECE, :] = line[...]
 
 
-def letters_kernel(piece, got, back, pair, letter):
-    for out in (pair, letter):
-        out[0:PIECE, :] = piece[...]
-        out[PIECE:PAIR, :] = got[...]
-    letter[PAIR:PAIR + MSG, :] = back[...]
-
-
-def near_kernel(pair, g1, g2, m3, out):
-    for i, m in enumerate((pair, g1, g2, m3)):
-        out[i * PAIR:(i + 1) * PAIR, :] = m[0:PAIR, :]
+def pair_kernel(piece, got, out):
+    out[0:PIECE, :] = piece[...]
+    out[PIECE:PAIR, :] = got[...]
+
+
+def near_kernel(pair, g1, g2, g3, out):
+    for i, m in enumerate((pair, g1, g2, g3)):
+        out[i * PAIR:(i + 1) * PAIR, :] = m[...]
 
 
 BLOCK = 192
+BATCH = 9
 
 
 def absorb(ctx, n, kv, qs, acc, top):
@@ -249,12 +248,18 @@
         v = kv[pl.ds(pl.multiple_of(SLOTS + base, 256), size), :]
         one = lax.broadcasted_iota(jnp.int32, (size, HD), 0) < length - base
         v = jnp.concatenate([v, jnp.where(one, 1.0, 0.0).astype(BF16)], 1)
-        for g, q in enumerate(qs):
-            for start in range(0, QR, BLOCK):
-                rows = slice(g * QR + start, g * QR + start + BLOCK)
-                s = lax.dot_general(
+        blocks = [(g, q, start) for g, q in enumerate(qs) for start in range(0, QR, BLOCK)]
+        for first in range(0, len(blocks), BATCH):
+            batch = blocks[first:first + BATCH]
+            scores = [
+                lax.dot_general(
                     q[start:start + BLOCK, :], k, (((1,), (1,)), ((), ())), preferred_element_type=F32
                 )
+                for g, q, start in batch
+            ]
+            weights = []
+            for (g, q, start), s in zip(batch, scores):
+                rows = slice(g * QR + start, g * QR + start + BLOCK)
                 old = top[rows, :]
                 new = jnp.maximum(old, jnp.max(s, axis=1, keepdims=True))
                 less = new
@@ -266,10 +271,12 @@
                     less = jnp.where(seen, new, -MASKED)
                 p = jnp.exp2((s - jnp.concatenate([less] * (size // HD), 1)) * EXP)
                 shrink = jnp.exp2((old - new) * EXP)
+                top[rows, :] = new
+                weights.append((rows, p.astype(BF16), shrink))
+            for rows, p, shrink in weights:
                 acc[rows, :] = acc[rows, :] * jnp.concatenate([shrink, shrink], 1) + jnp.dot(
-                    p.astype(BF16), v, preferred_element_type=F32
+                    p, v, preferred_element_type=F32
                 )
-                top[rows, :] = new
 
     rest = length % 512
     full = length // 512 + (rest > 256).astype(jnp.int32)
@@ -285,33 +292,33 @@
         chunk(full * 512, 256)
 
 
-def first_kernel(ctx, q0, q1, kv0, kv1, acc, top):
-    acc[...] = jnp.zeros_like(acc)
-    top[...] = jnp.full_like(top, FLOOR)
-    for n, kv in enumerate((kv0, kv1)):
-        absorb(ctx, n, kv, (q0, q1), acc, top)
-
-
-def second_kernel(ctx, q0, q1, kv2, kv3, acc0, top0, out0, out1, acc, top):
-    acc[...] = acc0[...]
-    top[...] = top0[...]
-    for n, kv in enumerate((kv2, kv3)):
-        absorb(ctx, n + 2, kv, (q0, q1), acc, top)
+def attend_kernel(ctx, *refs, groups, hosts, begin, end):
+    qs, kvs, refs = refs[:groups], refs[groups:groups + len(hosts)], refs[groups + len(hosts):]
+    before, refs = ((), refs) if begin else (refs[:2], refs[2:])
+    outs, (acc, top) = refs[:-2], refs[-2:]
+    acc[...] = jnp.zeros_like(acc) if begin else before[0][...]
+    top[...] = jnp.full_like(top, FLOOR) if begin else before[1][...]
+    for n, kv in zip(hosts, kvs):
+        absorb(ctx, n, kv, qs, acc, top)
+    if not end:
+        return
     diagonal = lax.broadcasted_iota(jnp.int32, (HD, HD), 0) == lax.broadcasted_iota(jnp.int32, (HD, HD), 1)
     index = lax.broadcasted_iota(jnp.int32, (16, HD), 0)
-    for g, out in enumerate((out0, out1)):
+    for g, out in enumerate(outs):
         rows = slice(g * QR, (g + 1) * QR)
         total = acc[rows, HD:]
-        some = total > 0.0
-        total = jnp.where(some, total, 1.0)
-        out[0:QR, :] = jnp.where(some, acc[rows, :HD] / total, 0.0).astype(BF16)
-        level = jnp.where(some, top[rows, :] * EXP + jnp.log2(total), FLOOR)
+        out[0:QR, :] = (acc[rows, :HD] / jnp.where(total > 0.0, total, 1.0)).astype(BF16)
         packed = jnp.zeros((16, HD), F32)
         for b in range(5):
-            block = level[b * HD:(b + 1) * HD, :]
-            if b == 4:
-                block = jnp.concatenate([block, jnp.zeros((HD - QR + PR, HD), F32)], 0)
-            line = jnp.sum(jnp.where(diagonal, block, 0.0), axis=0, keepdims=True)
+            low = g * QR + b * HD
+            lines = []
+            for ref, column in ((acc, HD), (top, 0)):
+                block = ref[low:low + min(HD, QR - b * HD), column:column + HD]
+                if b == 4:
+                    block = jnp.concatenate([block, jnp.zeros((HD - QR + PR, HD), F32)], 0)
+                lines.append(jnp.sum(jnp.where(diagonal, block, 0.0), axis=0, keepdims=True))
+            some = lines[0] > 0.0
+            line = jnp.where(some, lines[1] * EXP + jnp.log2(jnp.where(some, lines[0], 1.0)), FLOOR)
             for i in range(3):
                 piece = line.astype(BF16).astype(F32)
                 packed = jnp.where(index == 3 * b + i, piece, packed)
@@ -319,31 +326,21 @@
         out[QR:MSG, :] = packed.astype(BF16)
 
 
-STATE = ((2 * QR, 2 * HD), (2 * QR, HD))
-
-
-def cache_call(kernel, host, arrays, outs, scratch, name):
+def attend(host, qs, hosts, kvs, state=(), end=False):
     whole = pl.BlockSpec(memory_space=pltpu.VMEM)
+    shapes = ((len(qs) * QR, 2 * HD), (len(qs) * QR, HD))
+    outs = [((MSG, HD), BF16)] * len(qs) if end else [(x, F32) for x in shapes]
+    arrays = (*qs, *kvs, *state)
     return pl.pallas_call(
-        kernel,
+        functools.partial(attend_kernel, groups=len(qs), hosts=hosts, begin=not state, end=end),
         in_specs=[pl.BlockSpec(memory_space=pltpu.SMEM)] + [whole] * len(arrays),
         out_specs=[whole] * len(outs),
         out_shape=[jax.ShapeDtypeStruct(shape, dtype) for shape, dtype in outs],
-        scratch_shapes=[pltpu.VMEM(shape, F32) for shape in scratch],
-        compiler_params=vmem(8),
+        scratch_shapes=[pltpu.VMEM(shape, F32) for shape in shapes] if end else [],
+        compiler_params=vmem(16),
         cost_estimate=LIGHT,
-        name=name,
+        name="attend",
     )(host, *arrays)
-
-
-def cache_first(host, qs, kvs):
-    return cache_call(first_kernel, host, (*qs, *kvs), [(x, F32) for x in STATE], (), "cache_first")
-
-
-def cache_second(host, qs, kvs, state):
-    return cache_call(
-        second_kernel, host, (*qs, *kvs, *state), [((MSG, HD), BF16)] * 2, STATE, "cache_second"
-    )
 
 
 NEAR = 8
@@ -375,7 +372,7 @@
 
 
 def middle_kernel(q, m0, m1, m2, m3, near, own_kv, pos, out_d, value, level, keys, vals):
-    parts = ((m0, 0), (m1, 0), (m2, 0), (m3, PAIR))
+    parts = ((m0, 0), (m1, 0), (m2, 0), (m3, 0))
     where = lay_out(near, keys, vals)
     diagonal = lax.broadcasted_iota(jnp.int32, (HD, HD), 0) == lax.broadcasted_iota(jnp.int32, (HD, HD), 1)
 
@@ -446,43 +443,38 @@
     host = lax.axis_index("ctx").reshape(1)
     tp = lax.axis_index("tp").reshape(1)
     send, keep = project(tp, prompt_hidden, kv_weight)
-    got = move(send, XLOW)
     kv_own, kv_give, q_own, own_kv, line, pos = pack(
         tp, cache_lengths, dec_owner, prompt_pos, cache_k, cache_v, prompt_q, dec_q, dec_k, dec_v
     )
     kv_adj = move(kv_give, XADJ)
     kv_core = move(kv_own, CORE)
+    got = move(tie(send, kv_core), XLOW)
     q1 = move(q_own, Y1)
-    q3 = move(q_own, Y3)
+    q2, q3 = move(q_own, Y2), move(q_own, Y3)
 
     send, keep = halve(4, tp, keep, got)
     got = move(send, Z6)
-    q2 = move(q_own, Y2)
-    groups = ((q1, q2), (q_own, q3))
-    state0 = cache_first(tie(host, send), groups[0], [kv_own, kv_core])
-    got = tie(got, *state0)
+    others = (q1, q2, q3)
+    state = attend(tie(host, send), others, (0, 1), (kv_own, kv_core))
+    got = tie(got, *state)
     send, keep = halve(2, tp, keep, got)
     got = move(send, Z2)
     kv_diag = move(tie(kv_adj, send), CORE)
-    back0 = cache_second(tie(host, send), groups[0], [kv_adj, kv_diag], state0)
-    got = tie(got, *back0)
+    back = attend(tie(host, send), others, (2, 3), (kv_adj, kv_diag), state, end=True)
+    got = tie(got, *back)
     half = (2 * ROWS, HD)
     send, total = glue(add_kernel, (), (keep, got), ((half, BF16), (half, F32)), "add")
     got = move(send, Z1)
-    m2 = move(tie(back0[1], send), Y2)
-    state1 = cache_first(tie(host, send), groups[1], [kv_own, kv_core])
-    got = tie(got, *state1)
+    m2, m3 = move(tie(back[1], send), Y2), move(tie(back[2], send), Y3)
     piece, = glue(join_kernel, (), (total, got, line), (((PIECE, HD), BF16),), "join")
     got = move(piece, XFAR)
-    m1 = move(tie(back0[0], piece), Y1)
-    back1 = cache_second(tie(host, piece), groups[1], [kv_adj, kv_diag], state1)
-    got = tie(got, m1, m2, *back1)
-    mine, back3 = back1
-    pair, letter = glue(
-        letters_kernel, (), (piece, got, back3), (((PAIR, HD), BF16), ((PAIR + MSG, HD), BF16)), "letters"
-    )
-    g2, g1, m3 = move(pair, Y2), move(pair, Y1), move(letter, Y3)
-    near, = glue(near_kernel, (), (pair, g1, g2, m3), (((4 * PAIR, HD), BF16),), "near")
+    m1 = move(tie(back[0], piece), Y1)
+    state = attend(tie(host, piece), (q_own,), (0, 1), (kv_own, kv_core))
+    got = tie(got, m1, m2, m3, *state)
+    pair, = glue(pair_kernel, (), (piece, got), (((PAIR, HD), BF16),), "pair")
+    g2, g1, g3 = move(pair, Y2), move(pair, Y1), move(pair, Y3)
+    mine, = attend(tie(host, pair), (q_own,), (2, 3), (kv_adj, kv_diag), state, end=True)
+    near, = glue(near_kernel, (), (pair, g1, g2, tie(g3, mine)), (((4 * PAIR, HD), BF16),), "near")
     far = move(near, CORE)
     out_d, value, level = last_call(
         middle_kernel, (q_own, mine, m1, m2, m3, near, own_kv, pos),

time: 59.5 us -> 58.2 us (0.978); the launches traced: 59.3 us -> 57.2 us
  Pallas kernels: 20.9 us -> 16.6 us
  waiting for transfers between devices: 4.79 us -> 6.36 us
  starting transfers between devices: 32.1 us -> 32.8 us
    pallas_call x4, Pallas kernels: 15.2 us -> 11 us  [attend(): pl.pallas_call(functools.partial(attend_kernel, groups=len(qs), hosts=hos...]
    ppermute x17 -> x18, waiting for transfers between devices: 4.79 us -> 6.36 us  [move(): return lax.ppermute(x, ('ctx', 'tp'), pairs)]
    ppermute x17 -> x18, starting transfers between devices: 32.1 us -> 32.8 us  [move(): return lax.ppermute(x, ('ctx', 'tp'), pairs)]
  transfers between devices with their start and end apart: 17 -> 18, of which waited for: 4 -> 4; matrix products, arithmetic and copies ran while one was open for 0% -> 0% of each run, Pallas kernels for 30% -> 24%
where the time goes in v2:
time: 58.2 us; the launch traced here: 57.2 us
  starting transfers between devices  32.8 us (56%)
  Pallas kernels  16.6 us (29%)
  waiting for transfers between devices  6.36 us (11%)
  between operations  1.45 us (2%)
    ppermute x18, starting transfers between devices, move(): return lax.ppermute(x, ('ctx', 'tp'), pairs)  32.8 us
    pallas_call x4, Pallas kernels, attend(): pl.pallas_call(functools.partial(attend_kernel, groups=len(qs), hosts=hos...  11 us
    ppermute x18, waiting for transfers between devices, move(): return lax.ppermute(x, ('ctx', 'tp'), pairs)  6.36 us
    pallas_call x2, Pallas kernels, last_call(): pl.pallas_call(kernel, in_specs=[whole] * len(arrays), out_specs=[whole]...  2.95 us
    pallas_call x1, Pallas kernels, far_call(): pl.pallas_call(kernel, in_specs=[pl.BlockSpec(memory_space=pltpu.SMEM)] *...  1.67 us
  transfers between devices with their start and end apart: 18, of which 4 were waited for; matrix products, arithmetic and copies ran while one was open for 0% of the time, Pallas kernels for 24%

profile of v2, /device:TPU:1, one launch (start us, length us, event | category | flops | bytes accessed | tf_op | source)
XLA Modules:
  0.0 57.2 jit_solution(7067830865340265706)
XLA Ops:
  1.3 1.7 %pack.1 = (bf16[2064,128]{1,0:T(8,128)(2,1)S(1)}, bf16[2064,128]{1,0:T(8,128)(2,1)S(1)}, bf16[592,128]{1,0:T(8,128)(2,1)S(1)}, f32[16,128]{1,0:T(8,128)S(1)}, bf...) custom-call(s32[1]{0:T(128)} %bitcast.tp, s32[1]{0:T(128)S(6)} %copy.13.lengths, s32[8]{0:T(128)} %owner.1, s32[64]{0:T(128)} %pos.1, ...), custom_call_target="tpu_custom_call" | custom-call | flops 1 | bytes 1 | tf_op jit(solution)/shard_map/pack/pallas_call | solution.py:84
  3.0 3.3 %collective-permute-start = (bf16[2064,128]{1,0:T(8,128)(2,1)S(1)}, bf16[2064,128]{1,0:T(8,128)(2,1)S(1)}, u32[]{:S(2)}, u32[]{:S(2)}) collective-permute-start(bf16[2064,128]{1,0:T(8,128)(2,1)S(1)} %get-tuple-element.43.refs_3_.refs_1_), channel_id=1, source_target_pairs={{0,16},{1,17},{2,18},{3,19},{4,20},{5,21},{6,22},{7,23},{8,24},{9,... | collective-permute-start | bytes 1585160 | tf_op jit(solution)/shard_map/ppermute | solution.py:51
  6.3 0.8 %collective-permute-start.7 = (bf16[2064,128]{1,0:T(8,128)(2,1)S(1)}, bf16[2064,128]{1,0:T(8,128)(2,1)S(1)}, u32[]{:S(2)}, u32[]{:S(2)}) collective-permute-start(bf16[2064,128]{1,0:T(8,128)(2,1)S(1)} %get-tuple-element.54), channel_id=1, source_target_pairs={{0,40},{1,41},{2,42},{3,43},{4,44},{5,45},{6,46},{7,47},{8,32},{9,... | collective-permute-start | bytes 1585160 | tf_op jit(solution)/shard_map/ppermute | solution.py:51
  7.1 0.9 %project.1 = (bf16[4,128,128]{2,1,0:T(8,128)(2,1)S(1)}, f32[4,128,128]{2,1,0:T(8,128)S(1)}) custom-call(s32[1]{0:T(128)} %bitcast.tp, bf16[64,1024]{1,0:T(8,128)(2,1)S(1)} %copy-done.1, bf16[1024,2048]{1,0:T(8,128)(2,1)S(1)} %copy-done), custom_call_target="tpu_custom_call" | custom-call | tf_op jit(solution)/shard_map/project/pallas_call | solution.py:100
  8.1 2.8 %collective-permute-start.5 = (bf16[592,128]{1,0:T(8,128)(2,1)S(1)}, bf16[592,128]{1,0:T(8,128)(2,1)S(1)}, u32[]{:S(2)}, u32[]{:S(2)}) collective-permute-start(bf16[592,128]{1,0:T(8,128)(2,1)S(1)} %get-tuple-element.40.refs_0_.q), channel_id=1, source_target_pairs={{0,192},{1,193},{2,194},{3,195},{4,196},{5,197},{6,198},{7,199},{8... | collective-permute-start | bytes 454664 | tf_op jit(solution)/shard_map/ppermute | solution.py:51
  11.6 1.2 %collective-permute-done.1.got = bf16[4,128,128]{2,1,0:T(8,128)(2,1)S(1)} collective-permute-done((bf16[4,128,128]{2,1,0:T(8,128)(2,1)S(1)}, bf16[4,128,128]{2,1,0:T(8,128)(2,1)S(1)}, u32[]{:S(2)}, u32[]{:S(2)}) %collective-permute-start.1) | collective-permute-done | bytes 131104 | tf_op jit(solution)/shard_map/ppermute | solution.py:51
  12.8 6.1 %collective-permute-start.2 = (bf16[2,128,128]{2,1,0:T(8,128)(2,1)S(1)}, bf16[2,128,128]{2,1,0:T(8,128)(2,1)S(1)}, u32[]{:S(2)}, u32[]{:S(2)}) collective-permute-start(bf16[2,128,128]{2,1,0:T(8,128)(2,1)S(1)} %get-tuple-element.46), channel_id=1, source_target_pairs={{0,6},{1,7},{2,4},{3,5},{4,2},{5,3},{6,0},{7,1},{8,14},{9,15},{10,... | collective-permute-start | bytes 196616 | tf_op jit(solution)/shard_map/ppermute | solution.py:51
  19.0 3.8 %attend.4 = (f32[1728,256]{1,0:T(8,128)S(1)}, f32[1728,128]{1,0:T(8,128)S(1)}) custom-call(s32[1]{0:T(128)} %bitcast.1.ctx, bf16[592,128]{1,0:T(8,128)(2,1)S(1)} %collective-permute-done.3.refs_0_, bf16[592,128]{1,0:T(8,128)(2,1)S(1)} %collective-permute-done.4.refs_1_, bf16[592,128]{1,0:T(8,128)(2,1)S(1)} %collective-permute-done.5.refs_2_, ...), custom_call_target="tpu_custom_call" | custom-call | flops 1 | bytes 1 | tf_op jit(solution)/shard_map/attend/pallas_call | solution.py:334
  22.9 1.6 %collective-permute-start.8 = (bf16[2064,128]{1,0:T(8,128)(2,1)S(1)}, bf16[2064,128]{1,0:T(8,128)(2,1)S(1)}, u32[]{:S(2)}, u32[]{:S(2)}) collective-permute-start(bf16[2064,128]{1,0:T(8,128)(2,1)S(1)} %collective-permute-done.7.refs_3_.refs_1_), channel_id=1, source_target_pairs={{0,16},{1,17},{2,18},{3,19},{4,20},{5,21},{6,22},{7,23},{8,24},{9,... | collective-permute-start | bytes 1585160 | tf_op jit(solution)/shard_map/ppermute | solution.py:51
  24.4 2.6 %collective-permute-start.6 = (bf16[1,128,128]{2,1,0:T(8,128)(2,1)S(1)}, bf16[1,128,128]{2,1,0:T(8,128)(2,1)S(1)}, u32[]{:S(2)}, u32[]{:S(2)}) collective-permute-start(bf16[1,128,128]{2,1,0:T(8,128)(2,1)S(1)} %get-tuple-element.52), channel_id=1, source_target_pairs={{0,2},{1,3},{2,0},{3,1},{4,6},{5,7},{6,4},{7,5},{8,10},{9,11},{10,... | collective-permute-start | bytes 98312 | tf_op jit(solution)/shard_map/ppermute | solution.py:51
  27.0 3.3 %attend.5 = (bf16[592,128]{1,0:T(8,128)(2,1)S(1)}, bf16[592,128]{1,0:T(8,128)(2,1)S(1)}, bf16[592,128]{1,0:T(8,128)(2,1)S(1)}) custom-call(s32[1]{0:T(128)} %bitcast.1.ctx, bf16[592,128]{1,0:T(8,128)(2,1)S(1)} %collective-permute-done.3.refs_0_, bf16[592,128]{1,0:T(8,128)(2,1)S(1)} %collective-permute-done.4.refs_1_, ...), custom_call_target="tpu_custom_call" | custom-call | flops 1 | bytes 1 | tf_op jit(solution)/shard_map/attend/pallas_call | solution.py:334
  30.4 1.7 %collective-permute-start.9 = (bf16[128,128]{1,0:T(8,128)(2,1)S(1)}, bf16[128,128]{1,0:T(8,128)(2,1)S(1)}, u32[]{:S(2)}, u32[]{:S(2)}) collective-permute-start(bf16[128,128]{1,0:T(8,128)(2,1)S(1)} %get-tuple-element.61), channel_id=1, source_target_pairs={{0,1},{1,0},{2,3},{3,2},{4,5},{5,4},{6,7},{7,6},{8,9},{9,8},{10,11... | collective-permute-start | bytes 98312 | tf_op jit(solution)/shard_map/ppermute | solution.py:51
  32.1 5.4 %collective-permute-start.12 = (bf16[592,128]{1,0:T(8,128)(2,1)S(1)}, bf16[592,128]{1,0:T(8,128)(2,1)S(1)}, u32[]{:S(2)}, u32[]{:S(2)}) collective-permute-start(bf16[592,128]{1,0:T(8,128)(2,1)S(1)} %get-tuple-element.64), channel_id=1, source_target_pairs={{0,128},{1,129},{2,130},{3,131},{4,132},{5,133},{6,134},{7,135},{8... | collective-permute-start | bytes 454664 | tf_op jit(solution)/shard_map/ppermute | solution.py:51
  37.6 1.8 %collective-permute-start.10 = (bf16[144,128]{1,0:T(8,128)(2,1)S(1)}, bf16[144,128]{1,0:T(8,128)(2,1)S(1)}, u32[]{:S(2)}, u32[]{:S(2)}) collective-permute-start(bf16[144,128]{1,0:T(8,128)(2,1)S(1)} %join.1.piece), channel_id=1, source_target_pairs={{0,32},{1,33},{2,34},{3,35},{4,36},{5,37},{6,38},{7,39},{8,40},{9,... | collective-permute-start | bytes 110600 | tf_op jit(solution)/shard_map/ppermute | solution.py:51
  39.4 2.0 %attend.6 = (f32[576,256]{1,0:T(8,128)S(1)}, f32[576,128]{1,0:T(8,128)S(1)}) custom-call(s32[1]{0:T(128)} %bitcast.1.ctx, bf16[592,128]{1,0:T(8,128)(2,1)S(1)} %get-tuple-element.40.refs_0_.q, bf16[2064,128]{1,0:T(8,128)(2,1)S(1)} %get-tuple-element.43.refs_3_.refs_1_, bf16[2064,128]{1,0:T(8,128)(2,1)S(1)} %collective-permute-done.refs_4_.refs_2_), custom_call_target="tpu_custom_call" | custom-call | flops 1 | bytes 1 | tf_op jit(solution)/shard_map/attend/pallas_call | solution.py:334
  41.4 0.6 %collective-permute-done.10.got = bf16[144,128]{1,0:T(8,128)(2,1)S(1)} collective-permute-done((bf16[144,128]{1,0:T(8,128)(2,1)S(1)}, bf16[144,128]{1,0:T(8,128)(2,1)S(1)}, u32[]{:S(2)}, u32[]{:S(2)}) %collective-permute-start.10) | collective-permute-done | bytes 36896 | tf_op jit(solution)/shard_map/ppermute | solution.py:51
  42.0 2.3 %collective-permute-done.13.m3 = bf16[592,128]{1,0:T(8,128)(2,1)S(1)} collective-permute-done((bf16[592,128]{1,0:T(8,128)(2,1)S(1)}, bf16[592,128]{1,0:T(8,128)(2,1)S(1)}, u32[]{:S(2)}, u32[]{:S(2)}) %collective-permute-start.13) | collective-permute-done | bytes 151584 | tf_op jit(solution)/shard_map/ppermute | solution.py:51
  44.4 2.8 %collective-permute-start.16 = (bf16[288,128]{1,0:T(8,128)(2,1)S(1)}, bf16[288,128]{1,0:T(8,128)(2,1)S(1)}, u32[]{:S(2)}, u32[]{:S(2)}) collective-permute-start(bf16[288,128]{1,0:T(8,128)(2,1)S(1)} %pair.1), channel_id=1, source_target_pairs={{0,192},{1,193},{2,194},{3,195},{4,196},{5,197},{6,198},{7,199},{8... | collective-permute-start | bytes 221192 | tf_op jit(solution)/shard_map/ppermute | solution.py:51
  47.2 0.4 collective-permute-start.15
  47.8 1.9 %attend.7.m0 = bf16[592,128]{1,0:T(8,128)(2,1)S(1)} custom-call(s32[1]{0:T(128)} %bitcast.1.ctx, bf16[592,128]{1,0:T(8,128)(2,1)S(1)} %get-tuple-element.40.refs_0_.q, bf16[2064,128]{1,0:T(8,128)(2,1)S(1)} %collective-permute-done.7.refs_3_.refs_1_, bf16[2064,128]{1,0:T(8,128)(2,1)S(1)} %collective-permute-done.8.refs_4_.refs_2_, ...), custom_call_target="tpu_custom_call" | custom-call | flops 1 | bytes 1 | tf_op jit(solution)/shard_map/attend/pallas_call | solution.py:334
  49.7 2.2 %collective-permute-done.15.g2 = bf16[288,128]{1,0:T(8,128)(2,1)S(1)} collective-permute-done((bf16[288,128]{1,0:T(8,128)(2,1)S(1)}, bf16[288,128]{1,0:T(8,128)(2,1)S(1)}, u32[]{:S(2)}, u32[]{:S(2)}) %collective-permute-start.15) | collective-permute-done | bytes 73760 | tf_op jit(solution)/shard_map/ppermute | solution.py:51
  51.9 2.4 %collective-permute-start.17 = (bf16[1152,128]{1,0:T(8,128)(2,1)S(1)}, bf16[1152,128]{1,0:T(8,128)(2,1)S(1)}, u32[]{:S(2)}, u32[]{:S(2)}) collective-permute-start(bf16[1152,128]{1,0:T(8,128)(2,1)S(1)} %near.1), channel_id=1, source_target_pairs={{0,16},{1,17},{2,18},{3,19},{4,20},{5,21},{6,22},{7,23},{8,24},{9,... | collective-permute-start | bytes 884744 | tf_op jit(solution)/shard_map/ppermute | solution.py:51
  54.3 1.6 %middle.1 = (bf16[8,1024]{1,0:T(8,128)(2,1)}, f32[512,128]{1,0:T(8,128)S(1)}, f32[512,128]{1,0:T(8,128)S(1)}) custom-call(bf16[592,128]{1,0:T(8,128)(2,1)S(1)} %get-tuple-element.40.refs_0_.q, bf16[592,128]{1,0:T(8,128)(2,1)S(1)} %attend.7.m0, bf16[592,128]{1,0:T(8,128)(2,1)S(1)} %collective-permute-done.11.m1, ...), custom_call_target="tpu_custom_call" | custom-call | flops 1 | bytes 1 | tf_op jit(solution)/shard_map/middle/pallas_call | solution.py:427
  55.8 1.4 %final.1 = bf16[64,1024]{1,0:T(8,128)(2,1)} custom-call(bf16[592,128]{1,0:T(8,128)(2,1)S(1)} %get-tuple-element.40.refs_0_.q, bf16[1152,128]{1,0:T(8,128)(2,1)S(1)} %collective-permute-done.17.far, f32[512,128]{1,0:T(8,128)S(1)} %get-tuple-element.76.value, f32[512,128]{1,0:T(8,128)S(1)} %get-tuple-element.74.level, f32[64,128]{1,0:T(8,128)S(1)} %get-tuple-element.73.pos), custom_call_target="tpu_custom_call" | custom-call | flops 1 | bytes 1 | tf_op jit(solution)/shard_map/final/pallas_call | solution.py:427
  (30 shorter events, 1.3 us)
Async XLA Ops:
  1.3 5.8 %copy-start = (bf16[1024,2048]{1,0:T(8,128)(2,1)S(1)}, bf16[1024,2048]{1,0:T(8,128)(2,1)}, u32[]{:S(2)}) copy-start(bf16[1024,2048]{1,0:T(8,128)(2,1)} %w.1) | copy-start | bytes 12582916
  1.3 5.8 %copy-start.1 = (bf16[64,1024]{1,0:T(8,128)(2,1)S(1)}, bf16[64,1024]{1,0:T(8,128)(2,1)}, u32[]{:S(2)}) copy-start(bf16[64,1024]{1,0:T(8,128)(2,1)} %h.1) | copy-start | bytes 393220
  3.0 5.0 %collective-permute-start = (bf16[2064,128]{1,0:T(8,128)(2,1)S(1)}, bf16[2064,128]{1,0:T(8,128)(2,1)S(1)}, u32[]{:S(2)}, u32[]{:S(2)}) collective-permute-start(bf16[2064,128]{1,0:T(8,128)(2,1)S(1)} %get-tuple-element.43.refs_3_.refs_1_), channel_id=1, source_target_pairs={{0,16},{1,17},{2,18},{3,19},{4,20},{5,21},{6,22},{7,23},{8,24},{9,... | collective-permute-start | bytes 1585160 | tf_op jit(solution)/shard_map/ppermute | solution.py:51
  6.3 16.5 %collective-permute-start.7 = (bf16[2064,128]{1,0:T(8,128)(2,1)S(1)}, bf16[2064,128]{1,0:T(8,128)(2,1)S(1)}, u32[]{:S(2)}, u32[]{:S(2)}) collective-permute-start(bf16[2064,128]{1,0:T(8,128)(2,1)S(1)} %get-tuple-element.54), channel_id=1, source_target_pairs={{0,40},{1,41},{2,42},{3,43},{4,44},{5,45},{6,46},{7,47},{8,32},{9,... | collective-permute-start | bytes 1585160 | tf_op jit(solution)/shard_map/ppermute | solution.py:51
  8.0 4.8 %collective-permute-start.1 = (bf16[4,128,128]{2,1,0:T(8,128)(2,1)S(1)}, bf16[4,128,128]{2,1,0:T(8,128)(2,1)S(1)}, u32[]{:S(2)}, u32[]{:S(2)}) collective-permute-start(bf16[4,128,128]{2,1,0:T(8,128)(2,1)S(1)} %get-tuple-element.44), channel_id=1, source_target_pairs={{0,8},{1,9},{2,10},{3,11},{4,12},{5,13},{6,14},{7,15},{8,0},{9,1},... | collective-permute-start | bytes 393224 | tf_op jit(solution)/shard_map/ppermute | solution.py:51
  8.1 10.8 %collective-permute-start.5 = (bf16[592,128]{1,0:T(8,128)(2,1)S(1)}, bf16[592,128]{1,0:T(8,128)(2,1)S(1)}, u32[]{:S(2)}, u32[]{:S(2)}) collective-permute-start(bf16[592,128]{1,0:T(8,128)(2,1)S(1)} %get-tuple-element.40.refs_0_.q), channel_id=1, source_target_pairs={{0,192},{1,193},{2,194},{3,195},{4,196},{5,197},{6,198},{7,199},{8... | collective-permute-start | bytes 454664 | tf_op jit(solution)/shard_map/ppermute | solution.py:51
  10.9 8.0 %collective-permute-start.4 = (bf16[592,128]{1,0:T(8,128)(2,1)S(1)}, bf16[592,128]{1,0:T(8,128)(2,1)S(1)}, u32[]{:S(2)}, u32[]{:S(2)}) collective-permute-start(bf16[592,128]{1,0:T(8,128)(2,1)S(1)} %get-tuple-element.40.refs_0_.q), channel_id=1, source_target_pairs={{0,128},{1,129},{2,130},{3,131},{4,132},{5,133},{6,134},{7,135},{8... | collective-permute-start | bytes 454664 | tf_op jit(solution)/shard_map/ppermute | solution.py:51
  11.3 7.7 %collective-permute-start.3 = (bf16[592,128]{1,0:T(8,128)(2,1)S(1)}, bf16[592,128]{1,0:T(8,128)(2,1)S(1)}, u32[]{:S(2)}, u32[]{:S(2)}) collective-permute-start(bf16[592,128]{1,0:T(8,128)(2,1)S(1)} %get-tuple-element.40.refs_0_.q), channel_id=1, source_target_pairs={{0,64},{1,65},{2,66},{3,67},{4,68},{5,69},{6,70},{7,71},{8,72},{9,... | collective-permute-start | bytes 454664 | tf_op jit(solution)/shard_map/ppermute | solution.py:51
  12.8 10.0 %collective-permute-start.2 = (bf16[2,128,128]{2,1,0:T(8,128)(2,1)S(1)}, bf16[2,128,128]{2,1,0:T(8,128)(2,1)S(1)}, u32[]{:S(2)}, u32[]{:S(2)}) collective-permute-start(bf16[2,128,128]{2,1,0:T(8,128)(2,1)S(1)} %get-tuple-element.46), channel_id=1, source_target_pairs={{0,6},{1,7},{2,4},{3,5},{4,2},{5,3},{6,0},{7,1},{8,14},{9,15},{10,... | collective-permute-start | bytes 196616 | tf_op jit(solution)/shard_map/ppermute | solution.py:51
  22.9 4.2 %collective-permute-start.8 = (bf16[2064,128]{1,0:T(8,128)(2,1)S(1)}, bf16[2064,128]{1,0:T(8,128)(2,1)S(1)}, u32[]{:S(2)}, u32[]{:S(2)}) collective-permute-start(bf16[2064,128]{1,0:T(8,128)(2,1)S(1)} %collective-permute-done.7.refs_3_.refs_1_), channel_id=1, source_target_pairs={{0,16},{1,17},{2,18},{3,19},{4,20},{5,21},{6,22},{7,23},{8,24},{9,... | collective-permute-start | bytes 1585160 | tf_op jit(solution)/shard_map/ppermute | solution.py:51
  24.4 5.9 %collective-permute-start.6 = (bf16[1,128,128]{2,1,0:T(8,128)(2,1)S(1)}, bf16[1,128,128]{2,1,0:T(8,128)(2,1)S(1)}, u32[]{:S(2)}, u32[]{:S(2)}) collective-permute-start(bf16[1,128,128]{2,1,0:T(8,128)(2,1)S(1)} %get-tuple-element.52), channel_id=1, source_target_pairs={{0,2},{1,3},{2,0},{3,1},{4,6},{5,7},{6,4},{7,5},{8,10},{9,11},{10,... | collective-permute-start | bytes 98312 | tf_op jit(solution)/shard_map/ppermute | solution.py:51
  30.4 7.1 %collective-permute-start.9 = (bf16[128,128]{1,0:T(8,128)(2,1)S(1)}, bf16[128,128]{1,0:T(8,128)(2,1)S(1)}, u32[]{:S(2)}, u32[]{:S(2)}) collective-permute-start(bf16[128,128]{1,0:T(8,128)(2,1)S(1)} %get-tuple-element.61), channel_id=1, source_target_pairs={{0,1},{1,0},{2,3},{3,2},{4,5},{5,4},{6,7},{7,6},{8,9},{9,8},{10,11... | collective-permute-start | bytes 98312 | tf_op jit(solution)/shard_map/ppermute | solution.py:51
  32.1 9.9 %collective-permute-start.12 = (bf16[592,128]{1,0:T(8,128)(2,1)S(1)}, bf16[592,128]{1,0:T(8,128)(2,1)S(1)}, u32[]{:S(2)}, u32[]{:S(2)}) collective-permute-start(bf16[592,128]{1,0:T(8,128)(2,1)S(1)} %get-tuple-element.64), channel_id=1, source_target_pairs={{0,128},{1,129},{2,130},{3,131},{4,132},{5,133},{6,134},{7,135},{8... | collective-permute-start | bytes 454664 | tf_op jit(solution)/shard_map/ppermute | solution.py:51
  37.5 6.9 %collective-permute-start.13 = (bf16[592,128]{1,0:T(8,128)(2,1)S(1)}, bf16[592,128]{1,0:T(8,128)(2,1)S(1)}, u32[]{:S(2)}, u32[]{:S(2)}) collective-permute-start(bf16[592,128]{1,0:T(8,128)(2,1)S(1)} %get-tuple-element.65), channel_id=1, source_target_pairs={{0,192},{1,193},{2,194},{3,195},{4,196},{5,197},{6,198},{7,199},{8... | collective-permute-start | bytes 454664 | tf_op jit(solution)/shard_map/ppermute | solution.py:51
  37.5 6.8 %collective-permute-start.11 = (bf16[592,128]{1,0:T(8,128)(2,1)S(1)}, bf16[592,128]{1,0:T(8,128)(2,1)S(1)}, u32[]{:S(2)}, u32[]{:S(2)}) collective-permute-start(bf16[592,128]{1,0:T(8,128)(2,1)S(1)} %get-tuple-element.63), channel_id=1, source_target_pairs={{0,64},{1,65},{2,66},{3,67},{4,68},{5,69},{6,70},{7,71},{8,72},{9,... | collective-permute-start | bytes 454664 | tf_op jit(solution)/shard_map/ppermute | solution.py:51
  37.6 4.4 %collective-permute-start.10 = (bf16[144,128]{1,0:T(8,128)(2,1)S(1)}, bf16[144,128]{1,0:T(8,128)(2,1)S(1)}, u32[]{:S(2)}, u32[]{:S(2)}) collective-permute-start(bf16[144,128]{1,0:T(8,128)(2,1)S(1)} %join.1.piece), channel_id=1, source_target_pairs={{0,32},{1,33},{2,34},{3,35},{4,36},{5,37},{6,38},{7,39},{8,40},{9,... | collective-permute-start | bytes 110600 | tf_op jit(solution)/shard_map/ppermute | solution.py:51
  44.4 5.3 %collective-permute-start.16 = (bf16[288,128]{1,0:T(8,128)(2,1)S(1)}, bf16[288,128]{1,0:T(8,128)(2,1)S(1)}, u32[]{:S(2)}, u32[]{:S(2)}) collective-permute-start(bf16[288,128]{1,0:T(8,128)(2,1)S(1)} %pair.1), channel_id=1, source_target_pairs={{0,192},{1,193},{2,194},{3,195},{4,196},{5,197},{6,198},{7,199},{8... | collective-permute-start | bytes 221192 | tf_op jit(solution)/shard_map/ppermute | solution.py:51
  47.2 4.7 %collective-permute-start.15 = (bf16[288,128]{1,0:T(8,128)(2,1)S(1)}, bf16[288,128]{1,0:T(8,128)(2,1)S(1)}, u32[]{:S(2)}, u32[]{:S(2)}) collective-permute-start(bf16[288,128]{1,0:T(8,128)(2,1)S(1)} %pair.1), channel_id=1, source_target_pairs={{0,128},{1,129},{2,130},{3,131},{4,132},{5,133},{6,134},{7,135},{8... | collective-permute-start | bytes 221192 | tf_op jit(solution)/shard_map/ppermute | solution.py:51
  47.6 4.3 %collective-permute-start.14 = (bf16[288,128]{1,0:T(8,128)(2,1)S(1)}, bf16[288,128]{1,0:T(8,128)(2,1)S(1)}, u32[]{:S(2)}, u32[]{:S(2)}) collective-permute-start(bf16[288,128]{1,0:T(8,128)(2,1)S(1)} %pair.1), channel_id=1, source_target_pairs={{0,64},{1,65},{2,66},{3,67},{4,68},{5,69},{6,70},{7,71},{8,72},{9,... | collective-permute-start | bytes 221192 | tf_op jit(solution)/shard_map/ppermute | solution.py:51
  51.9 3.9 %collective-permute-start.17 = (bf16[1152,128]{1,0:T(8,128)(2,1)S(1)}, bf16[1152,128]{1,0:T(8,128)(2,1)S(1)}, u32[]{:S(2)}, u32[]{:S(2)}) collective-permute-start(bf16[1152,128]{1,0:T(8,128)(2,1)S(1)} %near.1), channel_id=1, source_target_pairs={{0,16},{1,17},{2,18},{3,19},{4,20},{5,21},{6,22},{7,23},{8,24},{9,... | collective-permute-start | bytes 884744 | tf_op jit(solution)/shard_map/ppermute | solution.py:51

commit v3 on v2

--- a/solution.py
+++ b/solution.py
@@ -235,7 +235,7 @@
 
 
 BLOCK = 192
-BATCH = 9
+BATCH = 5
 
 
 def absorb(ctx, n, kv, qs, acc, top):
@@ -465,12 +465,12 @@
     half = (2 * ROWS, HD)
     send, total = glue(add_kernel, (), (keep, got), ((half, BF16), (half, F32)), "add")
     got = move(send, Z1)
-    m2, m3 = move(tie(back[1], send), Y2), move(tie(back[2], send), Y3)
+    m3, m2 = move(tie(back[2], send), Y3), move(tie(back[1], send), Y2)
     piece, = glue(join_kernel, (), (total, got, line), (((PIECE, HD), BF16),), "join")
     got = move(piece, XFAR)
     m1 = move(tie(back[0], piece), Y1)
     state = attend(tie(host, piece), (q_own,), (0, 1), (kv_own, kv_core))
-    got = tie(got, m1, m2, m3, *state)
+    got = tie(got, m3, m1, m2, *state)
     pair, = glue(pair_kernel, (), (piece, got), (((PAIR, HD), BF16),), "pair")
     g2, g1, g3 = move(pair, Y2), move(pair, Y1), move(pair, Y3)
     mine, = attend(tie(host, pair), (q_own,), (2, 3), (kv_adj, kv_diag), state, end=True)

time: 58.2 us -> 58.1 us (level); the launches traced: 57.2 us -> 58.8 us
  Pallas kernels: 16.6 us -> 20.4 us
  starting transfers between devices: 32.8 us -> 31.5 us
  waiting for transfers between devices: 6.36 us -> 5.4 us
    pallas_call x4, Pallas kernels: 11 us -> 14.8 us  [attend(): pl.pallas_call(functools.partial(attend_kernel, groups=len(qs), hosts=hos...]
    ppermute x18, starting transfers between devices: 32.8 us -> 31.5 us  [move(): return lax.ppermute(x, ('ctx', 'tp'), pairs)]
    ppermute x18, waiting for transfers between devices: 6.36 us -> 5.4 us  [move(): return lax.ppermute(x, ('ctx', 'tp'), pairs)]
  transfers between devices with their start and end apart: 18 -> 18, of which waited for: 4 -> 5; matrix products, arithmetic and copies ran while one was open for 0% -> 0% of each run, Pallas kernels for 24% -> 30%
where the time goes in v3:
time: 58.1 us; the launch traced here: 58.8 us
  starting transfers between devices  31.5 us (54%)
  Pallas kernels  20.4 us (35%)
  waiting for transfers between devices  5.4 us (9%)
  between operations  1.44 us (2%)
    ppermute x18, starting transfers between devices, move(): return lax.ppermute(x, ('ctx', 'tp'), pairs)  31.5 us
    pallas_call x4, Pallas kernels, attend(): pl.pallas_call(functools.partial(attend_kernel, groups=len(qs), hosts=hos...  14.8 us
    ppermute x18, waiting for transfers between devices, move(): return lax.ppermute(x, ('ctx', 'tp'), pairs)  5.4 us
    pallas_call x2, Pallas kernels, last_call(): pl.pallas_call(kernel, in_specs=[whole] * len(arrays), out_specs=[whole]...  2.95 us
    pallas_call x1, Pallas kernels, far_call(): pl.pallas_call(kernel, in_specs=[pl.BlockSpec(memory_space=pltpu.SMEM)] *...  1.67 us
  transfers between devices with their start and end apart: 18, of which 5 were waited for; matrix products, arithmetic and copies ran while one was open for 0% of the time, Pallas kernels for 30%

profile of v3, /device:TPU:1, one launch (start us, length us, event | category | flops | bytes accessed | tf_op | source)
XLA Modules:
  0.0 58.8 jit_solution(15332318047197940244)
XLA Ops:
  1.3 1.7 %pack.1 = (bf16[2064,128]{1,0:T(8,128)(2,1)S(1)}, bf16[2064,128]{1,0:T(8,128)(2,1)S(1)}, bf16[592,128]{1,0:T(8,128)(2,1)S(1)}, f32[16,128]{1,0:T(8,128)S(1)}, bf...) custom-call(s32[1]{0:T(128)} %bitcast.tp, s32[1]{0:T(128)S(6)} %copy.13.lengths, s32[8]{0:T(128)} %owner.1, s32[64]{0:T(128)} %pos.1, ...), custom_call_target="tpu_custom_call" | custom-call | flops 1 | bytes 1 | tf_op jit(solution)/shard_map/pack/pallas_call | solution.py:84
  3.0 3.3 %collective-permute-start = (bf16[2064,128]{1,0:T(8,128)(2,1)S(1)}, bf16[2064,128]{1,0:T(8,128)(2,1)S(1)}, u32[]{:S(2)}, u32[]{:S(2)}) collective-permute-start(bf16[2064,128]{1,0:T(8,128)(2,1)S(1)} %get-tuple-element.43.refs_3_.refs_1_), channel_id=1, source_target_pairs={{0,16},{1,17},{2,18},{3,19},{4,20},{5,21},{6,22},{7,23},{8,24},{9,... | collective-permute-start | bytes 1585160 | tf_op jit(solution)/shard_map/ppermute | solution.py:51
  6.3 0.8 %collective-permute-start.7 = (bf16[2064,128]{1,0:T(8,128)(2,1)S(1)}, bf16[2064,128]{1,0:T(8,128)(2,1)S(1)}, u32[]{:S(2)}, u32[]{:S(2)}) collective-permute-start(bf16[2064,128]{1,0:T(8,128)(2,1)S(1)} %get-tuple-element.54), channel_id=1, source_target_pairs={{0,40},{1,41},{2,42},{3,43},{4,44},{5,45},{6,46},{7,47},{8,32},{9,... | collective-permute-start | bytes 1585160 | tf_op jit(solution)/shard_map/ppermute | solution.py:51
  7.1 0.9 %project.1 = (bf16[4,128,128]{2,1,0:T(8,128)(2,1)S(1)}, f32[4,128,128]{2,1,0:T(8,128)S(1)}) custom-call(s32[1]{0:T(128)} %bitcast.tp, bf16[64,1024]{1,0:T(8,128)(2,1)S(1)} %copy-done.1, bf16[1024,2048]{1,0:T(8,128)(2,1)S(1)} %copy-done), custom_call_target="tpu_custom_call" | custom-call | tf_op jit(solution)/shard_map/project/pallas_call | solution.py:100
  8.1 2.8 %collective-permute-start.5 = (bf16[592,128]{1,0:T(8,128)(2,1)S(1)}, bf16[592,128]{1,0:T(8,128)(2,1)S(1)}, u32[]{:S(2)}, u32[]{:S(2)}) collective-permute-start(bf16[592,128]{1,0:T(8,128)(2,1)S(1)} %get-tuple-element.40.refs_0_.q), channel_id=1, source_target_pairs={{0,192},{1,193},{2,194},{3,195},{4,196},{5,197},{6,198},{7,199},{8... | collective-permute-start | bytes 454664 | tf_op jit(solution)/shard_map/ppermute | solution.py:51
  11.6 1.2 %collective-permute-done.1.got = bf16[4,128,128]{2,1,0:T(8,128)(2,1)S(1)} collective-permute-done((bf16[4,128,128]{2,1,0:T(8,128)(2,1)S(1)}, bf16[4,128,128]{2,1,0:T(8,128)(2,1)S(1)}, u32[]{:S(2)}, u32[]{:S(2)}) %collective-permute-start.1) | collective-permute-done | bytes 131104 | tf_op jit(solution)/shard_map/ppermute | solution.py:51
  12.8 6.1 %collective-permute-start.2 = (bf16[2,128,128]{2,1,0:T(8,128)(2,1)S(1)}, bf16[2,128,128]{2,1,0:T(8,128)(2,1)S(1)}, u32[]{:S(2)}, u32[]{:S(2)}) collective-permute-start(bf16[2,128,128]{2,1,0:T(8,128)(2,1)S(1)} %get-tuple-element.46), channel_id=1, source_target_pairs={{0,6},{1,7},{2,4},{3,5},{4,2},{5,3},{6,0},{7,1},{8,14},{9,15},{10,... | collective-permute-start | bytes 196616 | tf_op jit(solution)/shard_map/ppermute | solution.py:51
  19.0 4.5 %attend.4 = (f32[1728,256]{1,0:T(8,128)S(1)}, f32[1728,128]{1,0:T(8,128)S(1)}) custom-call(s32[1]{0:T(128)} %bitcast.1.ctx, bf16[592,128]{1,0:T(8,128)(2,1)S(1)} %collective-permute-done.3.refs_0_, bf16[592,128]{1,0:T(8,128)(2,1)S(1)} %collective-permute-done.4.refs_1_, bf16[592,128]{1,0:T(8,128)(2,1)S(1)} %collective-permute-done.5.refs_2_, ...), custom_call_target="tpu_custom_call" | custom-call | flops 1 | bytes 1 | tf_op jit(solution)/shard_map/attend/pallas_call | solution.py:334
  23.5 1.5 %collective-permute-start.8 = (bf16[2064,128]{1,0:T(8,128)(2,1)S(1)}, bf16[2064,128]{1,0:T(8,128)(2,1)S(1)}, u32[]{:S(2)}, u32[]{:S(2)}) collective-permute-start(bf16[2064,128]{1,0:T(8,128)(2,1)S(1)} %collective-permute-done.7.refs_3_.refs_1_), channel_id=1, source_target_pairs={{0,16},{1,17},{2,18},{3,19},{4,20},{5,21},{6,22},{7,23},{8,24},{9,... | collective-permute-start | bytes 1585160 | tf_op jit(solution)/shard_map/ppermute | solution.py:51
  25.1 2.6 %collective-permute-start.6 = (bf16[1,128,128]{2,1,0:T(8,128)(2,1)S(1)}, bf16[1,128,128]{2,1,0:T(8,128)(2,1)S(1)}, u32[]{:S(2)}, u32[]{:S(2)}) collective-permute-start(bf16[1,128,128]{2,1,0:T(8,128)(2,1)S(1)} %get-tuple-element.52), channel_id=1, source_target_pairs={{0,2},{1,3},{2,0},{3,1},{4,6},{5,7},{6,4},{7,5},{8,10},{9,11},{10,... | collective-permute-start | bytes 98312 | tf_op jit(solution)/shard_map/ppermute | solution.py:51
  27.7 5.3 %attend.5 = (bf16[592,128]{1,0:T(8,128)(2,1)S(1)}, bf16[592,128]{1,0:T(8,128)(2,1)S(1)}, bf16[592,128]{1,0:T(8,128)(2,1)S(1)}) custom-call(s32[1]{0:T(128)} %bitcast.1.ctx, bf16[592,128]{1,0:T(8,128)(2,1)S(1)} %collective-permute-done.3.refs_0_, bf16[592,128]{1,0:T(8,128)(2,1)S(1)} %collective-permute-done.4.refs_1_, ...), custom_call_target="tpu_custom_call" | custom-call | flops 1 | bytes 1 | tf_op jit(solution)/shard_map/attend/pallas_call | solution.py:334
  33.1 1.7 %collective-permute-start.9 = (bf16[128,128]{1,0:T(8,128)(2,1)S(1)}, bf16[128,128]{1,0:T(8,128)(2,1)S(1)}, u32[]{:S(2)}, u32[]{:S(2)}) collective-permute-start(bf16[128,128]{1,0:T(8,128)(2,1)S(1)} %get-tuple-element.61), channel_id=1, source_target_pairs={{0,1},{1,0},{2,3},{3,2},{4,5},{5,4},{6,7},{7,6},{8,9},{9,8},{10,11... | collective-permute-start | bytes 98312 | tf_op jit(solution)/shard_map/ppermute | solution.py:51
  34.8 3.3 %collective-permute-start.11 = (bf16[592,128]{1,0:T(8,128)(2,1)S(1)}, bf16[592,128]{1,0:T(8,128)(2,1)S(1)}, u32[]{:S(2)}, u32[]{:S(2)}) collective-permute-start(bf16[592,128]{1,0:T(8,128)(2,1)S(1)} %get-tuple-element.63), channel_id=1, source_target_pairs={{0,192},{1,193},{2,194},{3,195},{4,196},{5,197},{6,198},{7,199},{8... | collective-permute-start | bytes 454664 | tf_op jit(solution)/shard_map/ppermute | solution.py:51
  38.8 1.6 %collective-permute-start.10 = (bf16[144,128]{1,0:T(8,128)(2,1)S(1)}, bf16[144,128]{1,0:T(8,128)(2,1)S(1)}, u32[]{:S(2)}, u32[]{:S(2)}) collective-permute-start(bf16[144,128]{1,0:T(8,128)(2,1)S(1)} %join.1.piece), channel_id=1, source_target_pairs={{0,32},{1,33},{2,34},{3,35},{4,36},{5,37},{6,38},{7,39},{8,40},{9,... | collective-permute-start | bytes 110600 | tf_op jit(solution)/shard_map/ppermute | solution.py:51
  40.4 2.2 %attend.6 = (f32[576,256]{1,0:T(8,128)S(1)}, f32[576,128]{1,0:T(8,128)S(1)}) custom-call(s32[1]{0:T(128)} %bitcast.1.ctx, bf16[592,128]{1,0:T(8,128)(2,1)S(1)} %get-tuple-element.40.refs_0_.q, bf16[2064,128]{1,0:T(8,128)(2,1)S(1)} %get-tuple-element.43.refs_3_.refs_1_, bf16[2064,128]{1,0:T(8,128)(2,1)S(1)} %collective-permute-done.refs_4_.refs_2_), custom_call_target="tpu_custom_call" | custom-call | flops 1 | bytes 1 | tf_op jit(solution)/shard_map/attend/pallas_call | solution.py:334
  43.1 1.6 %collective-permute-done.11.m3 = bf16[592,128]{1,0:T(8,128)(2,1)S(1)} collective-permute-done((bf16[592,128]{1,0:T(8,128)(2,1)S(1)}, bf16[592,128]{1,0:T(8,128)(2,1)S(1)}, u32[]{:S(2)}, u32[]{:S(2)}) %collective-permute-start.11) | collective-permute-done | bytes 151584 | tf_op jit(solution)/shard_map/ppermute | solution.py:51
  44.7 0.7 %collective-permute-done.12.m1 = bf16[592,128]{1,0:T(8,128)(2,1)S(1)} collective-permute-done((bf16[592,128]{1,0:T(8,128)(2,1)S(1)}, bf16[592,128]{1,0:T(8,128)(2,1)S(1)}, u32[]{:S(2)}, u32[]{:S(2)}) %collective-permute-start.12) | collective-permute-done | bytes 151584 | tf_op jit(solution)/shard_map/ppermute | solution.py:51
  45.4 2.8 %collective-permute-start.16 = (bf16[288,128]{1,0:T(8,128)(2,1)S(1)}, bf16[288,128]{1,0:T(8,128)(2,1)S(1)}, u32[]{:S(2)}, u32[]{:S(2)}) collective-permute-start(bf16[288,128]{1,0:T(8,128)(2,1)S(1)} %pair.1), channel_id=1, source_target_pairs={{0,192},{1,193},{2,194},{3,195},{4,196},{5,197},{6,198},{7,199},{8... | collective-permute-start | bytes 221192 | tf_op jit(solution)/shard_map/ppermute | solution.py:51
  48.2 0.7 %collective-permute-start.14 = (bf16[288,128]{1,0:T(8,128)(2,1)S(1)}, bf16[288,128]{1,0:T(8,128)(2,1)S(1)}, u32[]{:S(2)}, u32[]{:S(2)}) collective-permute-start(bf16[288,128]{1,0:T(8,128)(2,1)S(1)} %pair.1), channel_id=1, source_target_pairs={{0,64},{1,65},{2,66},{3,67},{4,68},{5,69},{6,70},{7,71},{8,72},{9,... | collective-permute-start | bytes 221192 | tf_op jit(solution)/shard_map/ppermute | solution.py:51
  48.9 2.8 %attend.7.m0 = bf16[592,128]{1,0:T(8,128)(2,1)S(1)} custom-call(s32[1]{0:T(128)} %bitcast.1.ctx, bf16[592,128]{1,0:T(8,128)(2,1)S(1)} %get-tuple-element.40.refs_0_.q, bf16[2064,128]{1,0:T(8,128)(2,1)S(1)} %collective-permute-done.7.refs_3_.refs_1_, bf16[2064,128]{1,0:T(8,128)(2,1)S(1)} %collective-permute-done.8.refs_4_.refs_2_, ...), custom_call_target="tpu_custom_call" | custom-call | flops 1 | bytes 1 | tf_op jit(solution)/shard_map/attend/pallas_call | solution.py:334
  51.7 1.4 %collective-permute-done.15.g2 = bf16[288,128]{1,0:T(8,128)(2,1)S(1)} collective-permute-done((bf16[288,128]{1,0:T(8,128)(2,1)S(1)}, bf16[288,128]{1,0:T(8,128)(2,1)S(1)}, u32[]{:S(2)}, u32[]{:S(2)}) %collective-permute-start.15) | collective-permute-done | bytes 73760 | tf_op jit(solution)/shard_map/ppermute | solution.py:51
  53.1 2.7 %collective-permute-start.17 = (bf16[1152,128]{1,0:T(8,128)(2,1)S(1)}, bf16[1152,128]{1,0:T(8,128)(2,1)S(1)}, u32[]{:S(2)}, u32[]{:S(2)}) collective-permute-start(bf16[1152,128]{1,0:T(8,128)(2,1)S(1)} %near.1), channel_id=1, source_target_pairs={{0,16},{1,17},{2,18},{3,19},{4,20},{5,21},{6,22},{7,23},{8,24},{9,... | collective-permute-start | bytes 884744 | tf_op jit(solution)/shard_map/ppermute | solution.py:51
  55.8 1.6 %middle.1 = (bf16[8,1024]{1,0:T(8,128)(2,1)}, f32[512,128]{1,0:T(8,128)S(1)}, f32[512,128]{1,0:T(8,128)S(1)}) custom-call(bf16[592,128]{1,0:T(8,128)(2,1)S(1)} %get-tuple-element.40.refs_0_.q, bf16[592,128]{1,0:T(8,128)(2,1)S(1)} %attend.7.m0, bf16[592,128]{1,0:T(8,128)(2,1)S(1)} %collective-permute-done.12.m1, ...), custom_call_target="tpu_custom_call" | custom-call | flops 1 | bytes 1 | tf_op jit(solution)/shard_map/middle/pallas_call | solution.py:427
  57.4 1.4 %final.1 = bf16[64,1024]{1,0:T(8,128)(2,1)} custom-call(bf16[592,128]{1,0:T(8,128)(2,1)S(1)} %get-tuple-element.40.refs_0_.q, bf16[1152,128]{1,0:T(8,128)(2,1)S(1)} %collective-permute-done.17.far, f32[512,128]{1,0:T(8,128)S(1)} %get-tuple-element.76.value, f32[512,128]{1,0:T(8,128)S(1)} %get-tuple-element.74.level, f32[64,128]{1,0:T(8,128)S(1)} %get-tuple-element.73.pos), custom_call_target="tpu_custom_call" | custom-call | flops 1 | bytes 1 | tf_op jit(solution)/shard_map/final/pallas_call | solution.py:427
  (30 shorter events, 2.1 us)
Async XLA Ops:
  1.3 5.8 %copy-start = (bf16[1024,2048]{1,0:T(8,128)(2,1)S(1)}, bf16[1024,2048]{1,0:T(8,128)(2,1)}, u32[]{:S(2)}) copy-start(bf16[1024,2048]{1,0:T(8,128)(2,1)} %w.1) | copy-start | bytes 12582916
  1.3 5.8 %copy-start.1 = (bf16[64,1024]{1,0:T(8,128)(2,1)S(1)}, bf16[64,1024]{1,0:T(8,128)(2,1)}, u32[]{:S(2)}) copy-start(bf16[64,1024]{1,0:T(8,128)(2,1)} %h.1) | copy-start | bytes 393220
  3.0 5.0 %collective-permute-start = (bf16[2064,128]{1,0:T(8,128)(2,1)S(1)}, bf16[2064,128]{1,0:T(8,128)(2,1)S(1)}, u32[]{:S(2)}, u32[]{:S(2)}) collective-permute-start(bf16[2064,128]{1,0:T(8,128)(2,1)S(1)} %get-tuple-element.43.refs_3_.refs_1_), channel_id=1, source_target_pairs={{0,16},{1,17},{2,18},{3,19},{4,20},{5,21},{6,22},{7,23},{8,24},{9,... | collective-permute-start | bytes 1585160 | tf_op jit(solution)/shard_map/ppermute | solution.py:51
  6.3 17.2 %collective-permute-start.7 = (bf16[2064,128]{1,0:T(8,128)(2,1)S(1)}, bf16[2064,128]{1,0:T(8,128)(2,1)S(1)}, u32[]{:S(2)}, u32[]{:S(2)}) collective-permute-start(bf16[2064,128]{1,0:T(8,128)(2,1)S(1)} %get-tuple-element.54), channel_id=1, source_target_pairs={{0,40},{1,41},{2,42},{3,43},{4,44},{5,45},{6,46},{7,47},{8,32},{9,... | collective-permute-start | bytes 1585160 | tf_op jit(solution)/shard_map/ppermute | solution.py:51
  8.0 4.8 %collective-permute-start.1 = (bf16[4,128,128]{2,1,0:T(8,128)(2,1)S(1)}, bf16[4,128,128]{2,1,0:T(8,128)(2,1)S(1)}, u32[]{:S(2)}, u32[]{:S(2)}) collective-permute-start(bf16[4,128,128]{2,1,0:T(8,128)(2,1)S(1)} %get-tuple-element.44), channel_id=1, source_target_pairs={{0,8},{1,9},{2,10},{3,11},{4,12},{5,13},{6,14},{7,15},{8,0},{9,1},... | collective-permute-start | bytes 393224 | tf_op jit(solution)/shard_map/ppermute | solution.py:51
  8.1 10.8 %collective-permute-start.5 = (bf16[592,128]{1,0:T(8,128)(2,1)S(1)}, bf16[592,128]{1,0:T(8,128)(2,1)S(1)}, u32[]{:S(2)}, u32[]{:S(2)}) collective-permute-start(bf16[592,128]{1,0:T(8,128)(2,1)S(1)} %get-tuple-element.40.refs_0_.q), channel_id=1, source_target_pairs={{0,192},{1,193},{2,194},{3,195},{4,196},{5,197},{6,198},{7,199},{8... | collective-permute-start | bytes 454664 | tf_op jit(solution)/shard_map/ppermute | solution.py:51
  10.9 8.0 %collective-permute-start.4 = (bf16[592,128]{1,0:T(8,128)(2,1)S(1)}, bf16[592,128]{1,0:T(8,128)(2,1)S(1)}, u32[]{:S(2)}, u32[]{:S(2)}) collective-permute-start(bf16[592,128]{1,0:T(8,128)(2,1)S(1)} %get-tuple-element.40.refs_0_.q), channel_id=1, source_target_pairs={{0,128},{1,129},{2,130},{3,131},{4,132},{5,133},{6,134},{7,135},{8... | collective-permute-start | bytes 454664 | tf_op jit(solution)/shard_map/ppermute | solution.py:51
  11.3 7.7 %collective-permute-start.3 = (bf16[592,128]{1,0:T(8,128)(2,1)S(1)}, bf16[592,128]{1,0:T(8,128)(2,1)S(1)}, u32[]{:S(2)}, u32[]{:S(2)}) collective-permute-start(bf16[592,128]{1,0:T(8,128)(2,1)S(1)} %get-tuple-element.40.refs_0_.q), channel_id=1, source_target_pairs={{0,64},{1,65},{2,66},{3,67},{4,68},{5,69},{6,70},{7,71},{8,72},{9,... | collective-permute-start | bytes 454664 | tf_op jit(solution)/shard_map/ppermute | solution.py:51
  12.8 10.7 %collective-permute-start.2 = (bf16[2,128,128]{2,1,0:T(8,128)(2,1)S(1)}, bf16[2,128,128]{2,1,0:T(8,128)(2,1)S(1)}, u32[]{:S(2)}, u32[]{:S(2)}) collective-permute-start(bf16[2,128,128]{2,1,0:T(8,128)(2,1)S(1)} %get-tuple-element.46), channel_id=1, source_target_pairs={{0,6},{1,7},{2,4},{3,5},{4,2},{5,3},{6,0},{7,1},{8,14},{9,15},{10,... | collective-permute-start | bytes 196616 | tf_op jit(solution)/shard_map/ppermute | solution.py:51
  23.5 4.2 %collective-permute-start.8 = (bf16[2064,128]{1,0:T(8,128)(2,1)S(1)}, bf16[2064,128]{1,0:T(8,128)(2,1)S(1)}, u32[]{:S(2)}, u32[]{:S(2)}) collective-permute-start(bf16[2064,128]{1,0:T(8,128)(2,1)S(1)} %collective-permute-done.7.refs_3_.refs_1_), channel_id=1, source_target_pairs={{0,16},{1,17},{2,18},{3,19},{4,20},{5,21},{6,22},{7,23},{8,24},{9,... | collective-permute-start | bytes 1585160 | tf_op jit(solution)/shard_map/ppermute | solution.py:51
  25.1 7.9 %collective-permute-start.6 = (bf16[1,128,128]{2,1,0:T(8,128)(2,1)S(1)}, bf16[1,128,128]{2,1,0:T(8,128)(2,1)S(1)}, u32[]{:S(2)}, u32[]{:S(2)}) collective-permute-start(bf16[1,128,128]{2,1,0:T(8,128)(2,1)S(1)} %get-tuple-element.52), channel_id=1, source_target_pairs={{0,2},{1,3},{2,0},{3,1},{4,6},{5,7},{6,4},{7,5},{8,10},{9,11},{10,... | collective-permute-start | bytes 98312 | tf_op jit(solution)/shard_map/ppermute | solution.py:51
  33.1 5.1 %collective-permute-start.9 = (bf16[128,128]{1,0:T(8,128)(2,1)S(1)}, bf16[128,128]{1,0:T(8,128)(2,1)S(1)}, u32[]{:S(2)}, u32[]{:S(2)}) collective-permute-start(bf16[128,128]{1,0:T(8,128)(2,1)S(1)} %get-tuple-element.61), channel_id=1, source_target_pairs={{0,1},{1,0},{2,3},{3,2},{4,5},{5,4},{6,7},{7,6},{8,9},{9,8},{10,11... | collective-permute-start | bytes 98312 | tf_op jit(solution)/shard_map/ppermute | solution.py:51
  34.8 9.9 %collective-permute-start.11 = (bf16[592,128]{1,0:T(8,128)(2,1)S(1)}, bf16[592,128]{1,0:T(8,128)(2,1)S(1)}, u32[]{:S(2)}, u32[]{:S(2)}) collective-permute-start(bf16[592,128]{1,0:T(8,128)(2,1)S(1)} %get-tuple-element.63), channel_id=1, source_target_pairs={{0,192},{1,193},{2,194},{3,195},{4,196},{5,197},{6,198},{7,199},{8... | collective-permute-start | bytes 454664 | tf_op jit(solution)/shard_map/ppermute | solution.py:51
  38.1 6.6 %collective-permute-start.13 = (bf16[592,128]{1,0:T(8,128)(2,1)S(1)}, bf16[592,128]{1,0:T(8,128)(2,1)S(1)}, u32[]{:S(2)}, u32[]{:S(2)}) collective-permute-start(bf16[592,128]{1,0:T(8,128)(2,1)S(1)} %get-tuple-element.65), channel_id=1, source_target_pairs={{0,128},{1,129},{2,130},{3,131},{4,132},{5,133},{6,134},{7,135},{8... | collective-permute-start | bytes 454664 | tf_op jit(solution)/shard_map/ppermute | solution.py:51
  38.1 7.3 %collective-permute-start.12 = (bf16[592,128]{1,0:T(8,128)(2,1)S(1)}, bf16[592,128]{1,0:T(8,128)(2,1)S(1)}, u32[]{:S(2)}, u32[]{:S(2)}) collective-permute-start(bf16[592,128]{1,0:T(8,128)(2,1)S(1)} %get-tuple-element.64), channel_id=1, source_target_pairs={{0,64},{1,65},{2,66},{3,67},{4,68},{5,69},{6,70},{7,71},{8,72},{9,... | collective-permute-start | bytes 454664 | tf_op jit(solution)/shard_map/ppermute | solution.py:51
  38.8 4.3 %collective-permute-start.10 = (bf16[144,128]{1,0:T(8,128)(2,1)S(1)}, bf16[144,128]{1,0:T(8,128)(2,1)S(1)}, u32[]{:S(2)}, u32[]{:S(2)}) collective-permute-start(bf16[144,128]{1,0:T(8,128)(2,1)S(1)} %join.1.piece), channel_id=1, source_target_pairs={{0,32},{1,33},{2,34},{3,35},{4,36},{5,37},{6,38},{7,39},{8,40},{9,... | collective-permute-start | bytes 110600 | tf_op jit(solution)/shard_map/ppermute | solution.py:51
  45.4 6.2 %collective-permute-start.16 = (bf16[288,128]{1,0:T(8,128)(2,1)S(1)}, bf16[288,128]{1,0:T(8,128)(2,1)S(1)}, u32[]{:S(2)}, u32[]{:S(2)}) collective-permute-start(bf16[288,128]{1,0:T(8,128)(2,1)S(1)} %pair.1), channel_id=1, source_target_pairs={{0,192},{1,193},{2,194},{3,195},{4,196},{5,197},{6,198},{7,199},{8... | collective-permute-start | bytes 221192 | tf_op jit(solution)/shard_map/ppermute | solution.py:51
  48.2 4.8 %collective-permute-start.15 = (bf16[288,128]{1,0:T(8,128)(2,1)S(1)}, bf16[288,128]{1,0:T(8,128)(2,1)S(1)}, u32[]{:S(2)}, u32[]{:S(2)}) collective-permute-start(bf16[288,128]{1,0:T(8,128)(2,1)S(1)} %pair.1), channel_id=1, source_target_pairs={{0,128},{1,129},{2,130},{3,131},{4,132},{5,133},{6,134},{7,135},{8... | collective-permute-start | bytes 221192 | tf_op jit(solution)/shard_map/ppermute | solution.py:51
  48.2 4.8 %collective-permute-start.14 = (bf16[288,128]{1,0:T(8,128)(2,1)S(1)}, bf16[288,128]{1,0:T(8,128)(2,1)S(1)}, u32[]{:S(2)}, u32[]{:S(2)}) collective-permute-start(bf16[288,128]{1,0:T(8,128)(2,1)S(1)} %pair.1), channel_id=1, source_target_pairs={{0,64},{1,65},{2,66},{3,67},{4,68},{5,69},{6,70},{7,71},{8,72},{9,... | collective-permute-start | bytes 221192 | tf_op jit(solution)/shard_map/ppermute | solution.py:51
  53.1 4.3 %collective-permute-start.17 = (bf16[1152,128]{1,0:T(8,128)(2,1)S(1)}, bf16[1152,128]{1,0:T(8,128)(2,1)S(1)}, u32[]{:S(2)}, u32[]{:S(2)}) collective-permute-start(bf16[1152,128]{1,0:T(8,128)(2,1)S(1)} %near.1), channel_id=1, source_target_pairs={{0,16},{1,17},{2,18},{3,19},{4,20},{5,21},{6,22},{7,23},{8,24},{9,... | collective-permute-start | bytes 884744 | tf_op jit(solution)/shard_map/ppermute | solution.py:51
